TPU v7x, 256 devices: a whole 4x4x8 slice. The times are simulated.
256 devices in a mesh: ctx: 32 (over x_hi, z, core), head: 8 (over y, x_lo).
Axes of the slice: x: 4 (x_hi: 2, x_lo: 2; x = x_hi * 2 + x_lo), y: 4, z: 8, core: 2. Of those that a mesh axis runs over, the one named last changes fastest.
Arguments:
- queries: bfloat16 [8192, 8192], P(('ctx', 'head')), may hold values from -5 to 5
- keys: bfloat16 [8192, 1024], P(('ctx', 'head')), may hold values from -5 to 5
- values: bfloat16 [8192, 1024], P(('ctx', 'head')), may hold values from -6 to 6
- output_gradient: bfloat16 [8192, 8192], P(('ctx', 'head')), may hold values from -6 to 6
- doc_lengths: int32 [4], replicated, may hold values from 1 to 4096, 8192 in all
- span_of: int32 [32], replicated, may hold values from 0 to 31, each once
Outputs:
- attended: bfloat16 [8192, 8192], P(('ctx', 'head'))
- query_grad: bfloat16 [8192, 8192], P(('ctx', 'head'))
- key_gradient: bfloat16 [8192, 1024], P(('ctx', 'head'))
- value_gradient: bfloat16 [8192, 1024], P(('ctx', 'head'))
Inputs may be any that keep to these rules, and one draw needn't show every extreme that they name: `doc_lengths`: the lengths sum to 8192 and the longest is exactly 4096. `span_of`: every span number appears once.
All inputs are finite; a program needn't handle non-finite values.
Results may differ from a plain program's by a relative error of at most 0.024.
Values may be sent and summed in bfloat16 or wider, within the bound.
A program may use at most 64 MiB of HBM per device.

v0:
```python
import jax
import jax.numpy as jnp
from jax import lax
from jax.sharding import PartitionSpec as P

QUERY_HEADS = 64
KEY_VALUE_HEADS = 8
HEAD_WIDTH = 128


NEG = -1e30


def passed_along(block, axis, distance):
    devices = range(lax.axis_size(axis))
    route = [((i - distance) % len(devices), i) for i in devices]
    return lax.ppermute(block, axis, route)


def doc_index(positions, doc_ends):
    return jnp.sum((positions[:, None] >= doc_ends[None, :]).astype(jnp.int32), axis=1)


def span_lookup(span_of, wanted):
    slots = jnp.arange(span_of.shape[0], dtype=jnp.int32)
    return jnp.sum(jnp.where(slots[None, :] == wanted[:, None], span_of[None, :], 0), axis=1)


def per_device(queries, keys, values, output_gradient, doc_lengths, span_of):
    q_rows, k_rows, v_rows, grad_rows = (
        lax.all_to_all(queries, "head", split_axis=1, concat_axis=0, tiled=True),
        lax.all_to_all(keys, "head", split_axis=1, concat_axis=0, tiled=True),
        lax.all_to_all(values, "head", split_axis=1, concat_axis=0, tiled=True),
        lax.all_to_all(output_gradient, "head", split_axis=1, concat_axis=0, tiled=True),
    )
    rows_dev = q_rows.shape[0]
    kv_heads = k_rows.shape[1] // HEAD_WIDTH
    heads_per_group = QUERY_HEADS // KEY_VALUE_HEADS
    score_scale = HEAD_WIDTH ** (-0.5)
    cycle_size = lax.axis_size("ctx")
    ctx_index = lax.axis_index("ctx")
    doc_ends = jnp.cumsum(doc_lengths)
    offsets = jnp.arange(rows_dev, dtype=jnp.int32)
    own_span = span_lookup(span_of, jnp.reshape(ctx_index, (1,)))[0]
    query_pos = own_span * rows_dev + offsets
    query_doc = doc_index(query_pos, doc_ends)
    query4 = q_rows.reshape(rows_dev, kv_heads, heads_per_group, HEAD_WIDTH)
    grad4 = grad_rows.reshape(rows_dev, kv_heads, heads_per_group, HEAD_WIDTH)
    kv_block = jnp.stack([k_rows, v_rows]).reshape(2, rows_dev, kv_heads, HEAD_WIDTH)

    def allowed_for(key_span):
        key_pos = key_span * rows_dev + offsets
        key_doc = doc_index(key_pos, doc_ends)
        return (key_pos[None, :] <= query_pos[:, None]) & (key_doc[None, :] == query_doc[:, None])

    def scores_for(block, allowed):
        raw = jnp.einsum("qngd,knd->ngqk", query4, block[0], preferred_element_type=jnp.float32)
        return jnp.where(allowed, raw * score_scale, NEG)

    def weights_for(block, allowed, log_total):
        scores = scores_for(block, allowed)
        return jnp.where(allowed, jnp.exp(scores - log_total), 0.0).astype(jnp.bfloat16)

    def keep_same(running):
        return running

    def add_stats(running, block, key_span):
        allowed = allowed_for(key_span)

        def live_stats(running):
            row_max, row_total = running
            scores = scores_for(block, allowed)
            new_max = jnp.maximum(row_max, jnp.max(scores, axis=3, keepdims=True))
            terms = jnp.where(allowed, jnp.exp(scores - new_max), 0.0)
            return (
                new_max,
                row_total * jnp.exp(row_max - new_max) + jnp.sum(terms, axis=3, keepdims=True),
            )

        return lax.cond(jnp.any(allowed), live_stats, keep_same, running)

    def add_output(outsum, block, key_span, log_total):
        allowed = allowed_for(key_span)

        def live_output(outsum):
            weights = weights_for(block, allowed, log_total)
            return outsum + jnp.einsum(
                "ngqk,knd->qngd", weights, block[1], preferred_element_type=jnp.float32
            )

        return lax.cond(jnp.any(allowed), live_output, keep_same, outsum)

    def grad_terms(block, key_span, log_total, row_delta):
        allowed = allowed_for(key_span)

        def live_grads(unused_arg):
            weights = weights_for(block, allowed, log_total)
            prob_grad = jnp.einsum(
                "qngd,knd->ngqk", grad4, block[1], preferred_element_type=jnp.float32
            )
            score_grad = (weights.astype(jnp.float32) * (prob_grad - row_delta)).astype(
                jnp.bfloat16
            )
            query_part = score_scale * jnp.einsum(
                "ngqk,knd->qngd", score_grad, block[0], preferred_element_type=jnp.float32
            )
            key_part = score_scale * jnp.einsum(
                "ngqk,qngd->knd", score_grad, query4, preferred_element_type=jnp.float32
            )
            value_part = jnp.einsum(
                "ngqk,qngd->knd", weights, grad4, preferred_element_type=jnp.float32
            )
            return (query_part, jnp.stack([key_part, value_part]))

        def no_grads(unused_arg):
            return (
                jnp.zeros((rows_dev, kv_heads, heads_per_group, HEAD_WIDTH), jnp.float32),
                jnp.zeros((2, rows_dev, kv_heads, HEAD_WIDTH), jnp.float32),
            )

        return lax.cond(jnp.any(allowed), live_grads, no_grads, 0)

    start_stats = (
        jnp.full((kv_heads, heads_per_group, rows_dev, 1), NEG, jnp.float32),
        jnp.zeros((kv_heads, heads_per_group, rows_dev, 1), jnp.float32),
    )
    first_stats = add_stats(start_stats, kv_block, own_span)

    def cycle_turn(carried, turn):
        block, running = carried
        block = passed_along(block, "ctx", 1)
        source = (ctx_index - turn) % cycle_size
        running = add_stats(running, block, span_lookup(span_of, jnp.reshape(source, (1,)))[0])
        return ((block, running), block)

    (last_block, stats), received = lax.scan(
        cycle_turn, (kv_block, first_stats), jnp.arange(1, cycle_size, dtype=jnp.int32)
    )
    blocks = jnp.concatenate([kv_block[None], received])
    sources = (ctx_index - jnp.arange(cycle_size, dtype=jnp.int32)) % cycle_size
    block_spans = span_lookup(span_of, sources)
    log_total = stats[0] + jnp.log(stats[1])

    def output_turn(turn, outsum):
        return add_output(outsum, blocks[turn], block_spans[turn], log_total)

    outsum = lax.fori_loop(
        0,
        cycle_size,
        output_turn,
        jnp.zeros((rows_dev, kv_heads, heads_per_group, HEAD_WIDTH), jnp.float32),
    )
    attended = outsum.astype(jnp.bfloat16)
    row_delta = jnp.einsum("qngd,qngd->ngq", grad4, attended, preferred_element_type=jnp.float32)[
        ..., None
    ]
    zeros_query = jnp.zeros((rows_dev, kv_heads, heads_per_group, HEAD_WIDTH), jnp.float32)

    def grad_turn(turn, carried):
        query_acc, kv_acc = carried
        query_part, kv_part = grad_terms(blocks[turn], block_spans[turn], log_total, row_delta)
        kv_acc = passed_along(kv_acc + kv_part, "ctx", 1)
        return (query_acc + query_part, kv_acc)

    query_acc, kv_acc = lax.fori_loop(
        0,
        cycle_size,
        grad_turn,
        (zeros_query, jnp.zeros((2, rows_dev, kv_heads, HEAD_WIDTH), jnp.float32)),
    )
    attended_rows = attended.reshape(rows_dev, kv_heads * heads_per_group * HEAD_WIDTH)
    query_grad = query_acc.astype(jnp.bfloat16).reshape(
        rows_dev, kv_heads * heads_per_group * HEAD_WIDTH
    )
    key_gradient = kv_acc[0].astype(jnp.bfloat16).reshape(rows_dev, kv_heads * HEAD_WIDTH)
    value_gradient = kv_acc[1].astype(jnp.bfloat16).reshape(rows_dev, kv_heads * HEAD_WIDTH)
    return (
        lax.all_to_all(attended_rows, "head", split_axis=0, concat_axis=1, tiled=True),
        lax.all_to_all(query_grad, "head", split_axis=0, concat_axis=1, tiled=True),
        lax.all_to_all(key_gradient, "head", split_axis=0, concat_axis=1, tiled=True),
        lax.all_to_all(value_gradient, "head", split_axis=0, concat_axis=1, tiled=True),
    )


def solution(mesh):
    in_specs = (
        P(("ctx", "head"), None),
        P(("ctx", "head"), None),
        P(("ctx", "head"), None),
        P(("ctx", "head"), None),
        P(),
        P(),
    )
    out_specs = (
        P(("ctx", "head"), None),
        P(("ctx", "head"), None),
        P(("ctx", "head"), None),
        P(("ctx", "head"), None),
    )
    return jax.shard_map(
        per_device, mesh=mesh, in_specs=in_specs, out_specs=out_specs, check_vma=False
    )
```

profile of v0, /device:TPU:4, one launch (start us, length us, event | category | flops | bytes accessed | tf_op | source)
XLA Modules:
  0.0 1033.7 jit_solution(13495762371326459398)
XLA Ops:
  42.3 275.6 %while.52 = (s32[]{:T(128)}, bf16[2,256,1,128]{3,1,2,0:T(8,128)(2,1)S(1)}, f32[1,8,256,1]{2,1,3,0:T(8,128)S(1)}, f32[1,8,256,1]{2,1,3,0:T(8,128)S(1)}, bf16[31,2...) while((s32[]{:T(128)}, ...), condition=%wide.region_16.17_spmd.clone, body=%wide.region_8.16_spmd.clone.sunk | while | flops 138681712 | bytes 6144600 | solution.py:136
  323.0 123.2 %while.53 = (s32[]{:T(128)}, f32[256,1,8,128]{0,3,2,1:T(8,128)S(1)}, s32[32]{0:T(128)}, s32[4]{0:T(128)S(1)}, s32[256]{0:T(256)S(1)}, /*index=5*/bf16[32,2,256,1...) while((s32[]{:T(128)}, ...), condition=%wide.region_23.24_spmd.clone, body=%wide.region_18.23_spmd.clone.sunk | while | flops 271584512 | bytes 2901227 | solution.py:147
  452.7 530.1 %while.54 = (s32[]{:T(128)}, f32[256,1,8,128]{0,3,2,1:T(8,128)S(1)}, f32[2,256,1,128]{3,1,2,0:T(8,128)}, s32[32]{0:T(128)}, s32[4]{0:T(128)S(1)}, /*index=5*/s32...) while((s32[]{:T(128)}, ...), condition=%wide.region_29.30_spmd.clone, body=%wide.region_24.29_spmd.clone.sunk | while | flops 677022976 | bytes 16607081 | solution.py:165
  463.0 9.3 collective-permute-done.1
  478.5 9.3 collective-permute-done.1
  494.0 9.3 collective-permute-done.1
  525.0 9.3 collective-permute-done.1
  545.3 9.3 collective-permute-done.1
  637.2 9.3 collective-permute-done.1
  652.8 9.3 collective-permute-done.1
  668.3 9.3 collective-permute-done.1
  683.8 9.3 collective-permute-done.1
  699.3 9.3 collective-permute-done.1
  730.3 9.3 collective-permute-done.1
  745.9 9.3 collective-permute-done.1
  766.1 9.3 collective-permute-done.1
  781.7 9.3 collective-permute-done.1
  797.2 9.3 collective-permute-done.1
  812.7 9.3 collective-permute-done.1
  848.5 9.3 collective-permute-done.1
  941.6 9.4 collective-permute-done.1
  972.7 9.4 collective-permute-done.1
  984.4 11.8 %all_to_all.134 = bf16[8,32,128]{2,1,0:T(8,128)(2,1)S(1)} all-to-all(bf16[8,32,128]{2,1,0:T(8,128)(2,1)S(1)} %bitcast.288), channel_id=1, replica_groups=mesh['ctx'=32,'head'=8] {'head'}, dimensions={0} | all-to-all | bytes 131072 | tf_op jit(solution)/shard_map/all_to_all | solution.py:181
  1011.0 9.8 all-to-all-done.5
  (1026 shorter events, 744.5 us)
Async XLA Ops:
  2.1 11.5 %all-to-all-start = ((bf16[32,8,128]{2,0,1:T(8,128)(2,1)}), bf16[32,8,128]{2,0,1:T(8,128)(2,1)S(1)}, u32[]{:S(2)}, u32[]{:S(2)}) async-start(bf16[32,8,128]{2,0,1:T(8,128)(2,1)} %copy_bitcast_fusion.5), calls=%async_computation | async-start | bytes 131072 | tf_op jit(solution)/shard_map/all_to_all | solution.py:32
  13.6 11.9 %all-to-all-start.1 = ((bf16[32,8,128]{2,0,1:T(8,128)(2,1)}), bf16[32,8,128]{2,0,1:T(8,128)(2,1)S(1)}, u32[]{:S(2)}, u32[]{:S(2)}) async-start(bf16[32,8,128]{2,0,1:T(8,128)(2,1)} %copy_bitcast_fusion.4), calls=%async_computation.1 | async-start | bytes 131072 | tf_op jit(solution)/shard_map/all_to_all | solution.py:33
  25.4 12.1 %all-to-all-start.2 = ((bf16[32,8,1024]{2,0,1:T(8,128)(2,1)}), bf16[32,8,1024]{2,0,1:T(8,128)(2,1)S(1)}, u32[]{:S(2)}, u32[]{:S(2)}) async-start(bf16[32,8,1024]{2,0,1:T(8,128)(2,1)} %bitcast.262), calls=%async_computation.2 | async-start | bytes 1048576 | tf_op jit(solution)/shard_map/all_to_all | solution.py:31
  37.6 412.6 %all-to-all-start.4 = ((bf16[32,8,1024]{2,0,1:T(8,128)(2,1)}), bf16[32,8,1024]{2,0,1:T(8,128)(2,1)S(1)}, u32[]{:S(2)}, u32[]{:S(2)}) async-start(bf16[32,8,1024]{2,0,1:T(8,128)(2,1)} %bitcast.261), calls=%async_computation.4 | async-start | bytes 1048576 | tf_op jit(solution)/shard_map/all_to_all | solution.py:34
  462.6 9.6 collective-permute-start.1
  478.2 9.6 collective-permute-start.1
  493.7 9.6 collective-permute-start.1
  509.2 9.6 collective-permute-start.1
  524.7 9.6 collective-permute-start.1
  545.0 9.6 collective-permute-start.1
  585.6 9.6 collective-permute-start.1
  636.9 9.6 collective-permute-start.1
  652.4 9.6 collective-permute-start.1
  667.9 9.6 collective-permute-start.1
  683.5 9.6 collective-permute-start.1
  699.0 9.6 collective-permute-start.1
  714.5 9.6 collective-permute-start.1
  730.0 9.6 collective-permute-start.1
  745.5 9.6 collective-permute-start.1
  941.3 9.7 collective-permute-start.1
  972.4 9.7 collective-permute-start.1
  996.2 9.9 all-to-all-start.6
  1006.1 14.6 %all-to-all-start.5 = ((bf16[8,32,1024]{2,1,0:T(8,128)(2,1)}), bf16[8,32,1024]{2,1,0:T(8,128)(2,1)S(1)}, u32[]{:S(2)}, u32[]{:S(2)}) async-start(bf16[8,32,1024]{2,1,0:T(8,128)(2,1)} %all_to_all.116), calls=%async_computation.5 | async-start | bytes 1048576 | tf_op jit(solution)/shard_map/all_to_all | solution.py:179
  1020.8 12.1 %all-to-all-start.3 = ((bf16[8,32,1024]{2,1,0:T(8,128)(2,1)}), bf16[8,32,1024]{2,1,0:T(8,128)(2,1)S(1)}, u32[]{:S(2)}, u32[]{:S(2)}) async-start(bf16[8,32,1024]{2,1,0:T(8,128)(2,1)} %all_to_all.109), calls=%async_computation.3 | async-start | bytes 1048576 | tf_op jit(solution)/shard_map/all_to_all | solution.py:178
  (82 other events, 485.5 us)
where the time goes:
time: 1040 us; the launch traced here: 1030 us
  waiting for transfers between devices  453 us (44%)
  other arithmetic  183 us (18%)
  local copies, waits for them, and re-layouts  159 us (15%)
  loops' own time  147 us (14%)
  matrix products  49.8 us (5%)
  starting transfers between devices  28.2 us (3%)
  blocking collectives  11.8 us (1%)
    ppermute x63, waiting for transfers between devices, passed_along(): return lax.ppermute(block, axis, route)  419 us
    another operation x1, loops' own time, per_device(): lax.scan(cycle_turn, (kv_block, first_stats), jnp.arange(1, cycle_size, d...  61.8 us
    add x32, other arithmetic, grad_turn(): kv_acc = passed_along(kv_acc + kv_part, 'ctx', 1)  53.9 us
    another operation x1, loops' own time, per_device(): lax.fori_loop(0, cycle_size, output_turn, jnp.zeros((rows_dev, kv_heads,...  42.7 us
    another operation x1, loops' own time, per_device(): lax.fori_loop(0, cycle_size, grad_turn, (zeros_query, jnp.zeros((2, rows_...  40.5 us
    dynamic_slice x32, local copies, waits for them, and re-layouts, grad_turn(): block_spans[turn]  39.8 us
    dynamic_slice x32, local copies, waits for them, and re-layouts, output_turn(): return add_output(outsum, blocks[turn], block_spans[turn], log_total)  39.7 us
    reduce_or x32, other arithmetic, grad_terms(): return lax.cond(jnp.any(allowed), live_grads, no_grads, 0)  25 us
  transfers between devices with their start and end apart: 70, of which 69 were waited for; matrix products, arithmetic and copies ran while one was open for 20% of the time, Pallas kernels for 0%

commit v1 on v0

v1 whole, which is shorter than its diff:
```python
import functools
import math

import jax
import jax.numpy as jnp
from jax import lax
from jax.experimental import pallas as pl
from jax.experimental.pallas import tpu as pltpu
from jax.sharding import PartitionSpec as P

N_CTX = 32
SPAN = 256
WIDTH = 128
UNIT_HEADS = 4
UNITS = 2
MAX_BLOCKS = 17
SCALE = WIDTH**-0.5
LOG2_SCALE = SCALE * math.log2(math.e)
NEG = -1e30


def attention_kernel(
    span_ref, len_ref, unit_ref, q_hbm, do_hbm, kv_hbm,
    o_hbm, dq_hbm, dkv_hbm,
    holder, q_v, do_v, kv_v, o_v, dq_v, acc, dkv_v, scores, probs,
    q_t, do_t, do_s, o_t, dq_t, top, total, sem, out_sem,
):
    load_q = pltpu.make_async_copy(q_hbm, q_v, sem.at[0])
    load_do = pltpu.make_async_copy(do_hbm, do_v, sem.at[1])
    load_kv = pltpu.make_async_copy(kv_hbm, kv_v, sem.at[2])
    load_q.start()
    load_kv.start()
    load_do.start()

    def note(c, _):
        holder[span_ref[c]] = c
        return 0

    lax.fori_loop(0, N_CTX, note, 0)

    def clear(c, _):
        acc[c] = jnp.zeros((2, SPAN, WIDTH), jnp.float32)
        return 0

    lax.fori_loop(0, N_CTX, clear, 0)
    load_q.wait()
    load_do.wait()
    load_kv.wait()

    ends = []
    running = jnp.int32(0)
    for j in range(4):
        running = running + len_ref[j]
        ends.append(running)

    def doc_start(pos):
        start = jnp.zeros_like(pos)
        for end in ends:
            start = jnp.where(pos >= end, end, start)
        return start

    def unit(u, _):
        span = span_ref[unit_ref[u]]
        first_pos = span * SPAN
        first_block = doc_start(first_pos) // SPAN
        last_start = doc_start(first_pos + (SPAN - 1))
        blocks = span - first_block + 1
        q_pos = first_pos + lax.broadcasted_iota(jnp.int32, (1, SPAN), 1)
        q_start = doc_start(q_pos)

        for h in range(UNIT_HEADS):
            cols = pl.ds(h * WIDTH, WIDTH)
            q_t[h] = q_v[u, :, cols].T
            do_t[h] = do_v[u, :, cols].T
            top[h] = jnp.full((8, SPAN), NEG, jnp.float32)
            total[h] = jnp.zeros((8, SPAN), jnp.float32)
            o_t[h] = jnp.zeros((WIDTH, SPAN), jnp.float32)
            dq_t[h] = jnp.zeros((WIDTH, SPAN), jnp.float32)

        def score_block(i, masked):
            t = first_block + i
            k = kv_v[holder[t], 0]
            if masked:
                k_pos = t * SPAN + lax.broadcasted_iota(jnp.int32, (SPAN, SPAN), 0)
                allowed = (k_pos <= q_pos) & (k_pos >= q_start)
            for h in range(UNIT_HEADS):
                s = jnp.dot(k, q_t[h], preferred_element_type=jnp.float32)
                if masked:
                    s = jnp.where(allowed, s, NEG)
                scores[i, h] = s
                top[h] = jnp.maximum(top[h], jnp.max(s.reshape(SPAN // 8, 8, SPAN), axis=0))

        def score_step(i, _):
            t = first_block + i
            edge = (t == span) | (t * SPAN < last_start)

            @pl.when(edge)
            def _():
                score_block(i, True)

            @pl.when(jnp.logical_not(edge))
            def _():
                score_block(i, False)

            return 0

        lax.fori_loop(0, blocks, score_step, 0)
        for h in range(UNIT_HEADS):
            top[h] = jnp.broadcast_to(jnp.max(top[h], axis=0, keepdims=True), (8, SPAN))

        def weight_step(i, _):
            v_t = kv_v[holder[first_block + i], 1].T
            for h in range(UNIT_HEADS):
                p = jnp.exp2((scores[i, h] - top[h, 0:1]) * LOG2_SCALE)
                total[h] += jnp.sum(p.reshape(SPAN // 8, 8, SPAN), axis=0)
                p = p.astype(jnp.bfloat16)
                probs[i, h] = p
                o_t[h] += jnp.dot(v_t, p, preferred_element_type=jnp.float32)
            return 0

        lax.fori_loop(0, blocks, weight_step, 0)

        for h in range(UNIT_HEADS):
            cols = pl.ds(h * WIDTH, WIDTH)
            inverse = 1.0 / jnp.sum(total[h], axis=0, keepdims=True)
            out = (o_t[h] * inverse).astype(jnp.bfloat16)
            o_v[u, :, cols] = out.T
            scaled = (do_t[h].astype(jnp.float32) * inverse).astype(jnp.bfloat16)
            do_t[h] = scaled
            do_s[h] = scaled.T
            delta = jnp.sum(scaled.astype(jnp.float32) * out.astype(jnp.float32), axis=0, keepdims=True)
            total[h] = jnp.broadcast_to(delta, (8, SPAN))

        def grad_step(i, _):
            c = holder[first_block + i]
            k = kv_v[c, 0]
            v = kv_v[c, 1]
            k_t = k.T
            dk = jnp.zeros((SPAN, WIDTH), jnp.float32)
            dv = jnp.zeros((SPAN, WIDTH), jnp.float32)
            for h in range(UNIT_HEADS):
                p = probs[i, h]
                dp = jnp.dot(v, do_t[h], preferred_element_type=jnp.float32)
                dv += jnp.dot(p, do_s[h], preferred_element_type=jnp.float32)
                ds = (p.astype(jnp.float32) * (dp - total[h, 0:1])).astype(jnp.bfloat16)
                dk += jnp.dot(ds, q_v[u, :, pl.ds(h * WIDTH, WIDTH)], preferred_element_type=jnp.float32)
                dq_t[h] += jnp.dot(k_t, ds, preferred_element_type=jnp.float32)
            acc[c, 0] += dk * SCALE
            acc[c, 1] += dv
            return 0

        lax.fori_loop(0, blocks, grad_step, 0)
        for h in range(UNIT_HEADS):
            dq_v[u, :, pl.ds(h * WIDTH, WIDTH)] = (dq_t[h] * SCALE).astype(jnp.bfloat16).T
        return 0

    lax.fori_loop(0, UNITS, unit, 0)
    save_o = pltpu.make_async_copy(o_v, o_hbm, out_sem.at[0])
    save_dq = pltpu.make_async_copy(dq_v, dq_hbm, out_sem.at[1])
    save_o.start()
    save_dq.start()

    def pack(c, _):
        dkv_v[c] = acc[c].astype(jnp.bfloat16)
        return 0

    lax.fori_loop(0, N_CTX, pack, 0)
    save_dkv = pltpu.make_async_copy(dkv_v, dkv_hbm, out_sem.at[2])
    save_dkv.start()
    save_o.wait()
    save_dq.wait()
    save_dkv.wait()


def attention(q, do, kv, span_of, doc_lengths, unit_ctx):
    rows = jax.ShapeDtypeStruct((UNITS, SPAN, UNIT_HEADS * WIDTH), jnp.bfloat16)
    blocks = jax.ShapeDtypeStruct((N_CTX, 2, SPAN, WIDTH), jnp.bfloat16)
    smem = pl.BlockSpec(memory_space=pltpu.SMEM)
    hbm = pl.BlockSpec(memory_space=pl.ANY)
    vmem = pltpu.VMEM
    head_t = (UNIT_HEADS, WIDTH, SPAN)
    return pl.pallas_call(
        attention_kernel,
        out_shape=(rows, rows, blocks),
        in_specs=[smem, smem, smem, hbm, hbm, hbm],
        out_specs=(hbm, hbm, hbm),
        scratch_shapes=[
            pltpu.SMEM((N_CTX,), jnp.int32),
            vmem(rows.shape, jnp.bfloat16),
            vmem(rows.shape, jnp.bfloat16),
            vmem(blocks.shape, jnp.bfloat16),
            vmem(rows.shape, jnp.bfloat16),
            vmem(rows.shape, jnp.bfloat16),
            vmem(blocks.shape, jnp.float32),
            vmem(blocks.shape, jnp.bfloat16),
            vmem((MAX_BLOCKS, UNIT_HEADS, SPAN, SPAN), jnp.float32),
            vmem((MAX_BLOCKS, UNIT_HEADS, SPAN, SPAN), jnp.bfloat16),
            vmem(head_t, jnp.bfloat16),
            vmem(head_t, jnp.bfloat16),
            vmem((UNIT_HEADS, SPAN, WIDTH), jnp.bfloat16),
            vmem(head_t, jnp.float32),
            vmem(head_t, jnp.float32),
            vmem((UNIT_HEADS, 8, SPAN), jnp.float32),
            vmem((UNIT_HEADS, 8, SPAN), jnp.float32),
            pltpu.SemaphoreType.DMA((3,)),
            pltpu.SemaphoreType.DMA((3,)),
        ],
        compiler_params=pltpu.CompilerParams(vmem_limit_bytes=60 * 1024 * 1024),
        name="attention",
    )(span_of, doc_lengths, unit_ctx, q, do, kv)


MESH_IDS = pl.DeviceIdType.MESH


def place(z_size):
    ctx, head = lax.axis_index("ctx"), lax.axis_index("head")
    return ctx, head, ctx // (2 * z_size), (ctx // 2) % z_size, ctx % 2


def meet(group, ctx, head, core, heads, others):
    barrier = pltpu.get_barrier_semaphore()
    base = ctx - core

    def greet(step, _):
        peer = (core * heads + head + step) % group
        pl.semaphore_signal(
            barrier, inc=1, device_id=(base + peer // heads, peer % heads), device_id_type=MESH_IDS
        )
        return 0

    lax.fori_loop(1, group, greet, 0)
    for other in others:
        pl.semaphore_signal(barrier, inc=1, device_id=(other, head), device_id_type=MESH_IDS)
    pl.semaphore_wait(barrier, group - 1 + len(others))


def arrived(ref, sem):
    pltpu.make_async_copy(ref, ref, sem).wait()


def send(src, dst, send_sem, recv_sem, ctx, head):
    pltpu.make_async_remote_copy(
        src_ref=src, dst_ref=dst, send_sem=send_sem, recv_sem=recv_sem,
        device_id=(ctx, head), device_id_type=MESH_IDS,
    ).start()


def gather_kernel(
    z_size, heads,
    q_in, do_in, k_in, v_in, q_out, do_out, kv_out,
    row_send, row_recv, piece_send, piece_recv, ring_send, right_recv, left_recv,
    cross_recv, twin_send, twin_recv, local_sem,
):
    ctx, head, x, z, core = place(z_size)
    group = 2 * heads
    base = ctx - core
    mine = core * heads + head
    wide = q_in.shape[1] // group

    def index(x_at, z_at):
        return (x_at * z_size + z_at) * 2 + core

    right, left = index(x, (z + 1) % z_size), index(x, (z + z_size - 1) % z_size)
    cross, twin = index(1 - x, z), base + 1 - core
    meet(group, ctx, head, core, heads, (right, left, cross))

    def piece_cols(at):
        return pl.ds(pl.multiple_of(at * WIDTH, WIDTH), WIDTH)

    def row_cols(at):
        peer_core, peer_head = at // heads, at % heads
        return pl.ds(pl.multiple_of((peer_head * 2 + peer_core) * wide, WIDTH), wide)

    def send_pieces(step, _):
        peer = (head + step) % heads
        for side, ref in enumerate((k_in, v_in)):
            send(
                ref.at[:, piece_cols(peer)], kv_out.at[ctx, side, head],
                piece_send, piece_recv, ctx, peer,
            )
        return 0

    lax.fori_loop(1, heads, send_pieces, 0)
    own = []
    for side, ref in enumerate((k_in, v_in)):
        own.append(
            pltpu.make_async_copy(ref.at[:, piece_cols(head)], kv_out.at[ctx, side, head], local_sem.at[side])
        )
        own[-1].start()

    def send_rows(src, dst, which):
        def step_rows(step, _):
            peer = (mine + step) % group
            send(
                src.at[:, row_cols(peer)], dst.at[mine],
                row_send.at[which], row_recv.at[which], base + peer // heads, peer % heads,
            )
            return 0

        lax.fori_loop(1, group, step_rows, 0)
        copy = pltpu.make_async_copy(src.at[:, row_cols(mine)], dst.at[mine], local_sem.at[2 + which])
        copy.start()
        own.append(copy)

    send_rows(q_in, q_out, 0)
    own[0].wait()
    own[1].wait()
    pieces = kv_out.at[ctx, :, pl.ds(0, heads - 1)]
    arrived(pieces, piece_recv)

    sent = []

    def forward(block, to, recv):
        sem = ring_send.at[len(sent)]
        send(kv_out.at[block], kv_out.at[block], sem, recv, to, head)
        sent.append((block, sem))

    def share(block):
        send(kv_out.at[block], kv_out.at[block], twin_send, twin_recv, twin, head)

    far = z_size // 2
    reach = ((far, far - 1), (far - 1, far))
    forward(ctx, cross, cross_recv)
    forward(ctx, right, right_recv.at[0, 0])
    forward(ctx, left, left_recv.at[0, 0])
    share(ctx)
    send_rows(do_in, do_out, 1)
    arrived(kv_out.at[cross], cross_recv)
    forward(cross, right, right_recv.at[1, 0])
    forward(cross, left, left_recv.at[1, 0])
    share(cross)
    for d in range(1, far + 1):
        for plane in range(2):
            at_x = x if plane == 0 else 1 - x
            for way in range(2):
                if d > reach[plane][way]:
                    continue
                recv, to = ((right_recv, right), (left_recv, left))[way]
                origin = (z + z_size - d) % z_size if way == 0 else (z + d) % z_size
                block = index(at_x, origin)
                arrived(kv_out.at[block], recv.at[plane, d - 1])
                if d < reach[plane][way]:
                    forward(block, to, recv.at[plane, d])
                share(block)

    arrived(pieces, piece_send)
    for block, sem in sent:
        arrived(kv_out.at[block], sem)
    half = kv_out.at[pl.ds(0, 2 * z_size)]
    arrived(half, twin_send)
    arrived(half, twin_recv)
    for which, dst in enumerate((q_out, do_out)):
        own[2 + which].wait()
        rows = dst.at[pl.ds(0, group - 1)]
        arrived(rows, row_send.at[which])
        arrived(rows, row_recv.at[which])


def gather(q, do, k, v, z_size, heads):
    tokens = q.shape[0]
    group = 2 * heads
    far = z_size // 2
    rows = jax.ShapeDtypeStruct((group, tokens, q.shape[1] // group), q.dtype)
    kv = jax.ShapeDtypeStruct((4 * z_size, 2, heads, tokens, WIDTH), q.dtype)
    hbm = pl.BlockSpec(memory_space=pl.ANY)
    dma = pltpu.SemaphoreType.DMA
    return pl.pallas_call(
        functools.partial(gather_kernel, z_size, heads),
        out_shape=(rows, rows, kv),
        in_specs=[hbm] * 4,
        out_specs=(hbm, hbm, hbm),
        scratch_shapes=[
            dma((2,)), dma((2,)), dma, dma, dma((4 * far - 2 + 1,)), dma((2, far)), dma((2, far)),
            dma, dma, dma, dma((4,)),
        ],
        compiler_params=pltpu.CompilerParams(collective_id=0, has_side_effects=True),
        name="gather",
    )(q, do, k, v)


def scatter_kernel(
    z_size, heads,
    o_in, dq_in, dkv_in, o_out, dq_out, dk_out, dv_out,
    part, twin_part, right_part, left_part, cross_part,
    row_send, row_recv, piece_send, piece_recv, ring_send, right_recv, left_recv,
    cross_recv, twin_send, twin_recv, local_sem,
):
    ctx, head, x, z, core = place(z_size)
    group = 2 * heads
    base = ctx - core
    mine = core * heads + head
    wide = o_in.shape[2]

    def index(x_at, z_at):
        return (x_at * z_size + z_at) * 2 + core

    right, left = index(x, (z + 1) % z_size), index(x, (z + z_size - 1) % z_size)
    cross, twin = index(1 - x, z), base + 1 - core
    meet(group, ctx, head, core, heads, (right, left, cross))

    load = pltpu.make_async_copy(dkv_in.at[:, core], part, local_sem.at[0])
    load.start()

    far = z_size // 2
    reach = ((far, far - 1), (far - 1, far))
    steps = []
    for back in range(far):
        for plane, way in ((0, 0), (1, 1), (1, 0), (0, 1)):
            d = reach[plane][way] - back
            if d > 0:
                steps.append((plane, way, d, back))

    def slot(plane, way, d):
        at_x = x if plane == 0 else 1 - x
        at_z = (z + d) % z_size if way == 0 else (z + z_size - d) % z_size
        return at_x * z_size + at_z

    order = [slot(plane, way, d) for plane, way, d, _ in steps]
    order += [slot(1, 0, 0), slot(0, 0, 0)]
    for n, block in enumerate(order):
        send(dkv_in.at[block, 1 - core], twin_part.at[block], twin_send, twin_recv.at[n], twin, head)

    def row_cols(at):
        return pl.ds(pl.multiple_of(((at % heads) * 2 + at // heads) * wide, WIDTH), wide)

    own = []

    def send_rows(src, dst, which):
        def step_rows(step, _):
            peer = (mine + step) % group
            send(
                src.at[peer], dst.at[:, row_cols_mine],
                row_send.at[which], row_recv.at[which], base + peer // heads, peer % heads,
            )
            return 0

        row_cols_mine = row_cols(mine)
        lax.fori_loop(1, group, step_rows, 0)
        copy = pltpu.make_async_copy(src.at[mine], dst.at[:, row_cols_mine], local_sem.at[1 + which])
        copy.start()
        own.append(copy)

    def combine(block, extras):
        def add_half(side, _):
            total = part[block, side].astype(jnp.float32) + twin_part[block, side].astype(jnp.float32)
            for ref, at in extras:
                total = total + ref[at + (side,)].astype(jnp.float32)
            part[block, side] = total.astype(part.dtype)
            return 0

        lax.fori_loop(0, 2, add_half, 0)

    load.wait()
    sent = []
    for n, (plane, way, d, back) in enumerate(steps):
        if n == min(4, len(steps) - 1):
            send_rows(o_in, o_out, 0)
        block = order[n]
        recv, buf, to = ((right_recv, right_part, right), (left_recv, left_part, left))[way]
        arrived(twin_part.at[block], twin_recv.at[n])
        extras = []
        if back > 0:
            arrived(buf.at[plane, back - 1], recv.at[plane, back - 1])
            extras = [(buf, (plane, back - 1))]
        combine(block, extras)
        send(part.at[block], buf.at[plane, back], ring_send.at[n], recv.at[plane, back], to, head)
        sent.append((block, ring_send.at[n]))
        if n == min(7, len(steps) - 1):
            send_rows(dq_in, dq_out, 1)
    for plane in (1, 0):
        n = len(steps) + 1 - plane
        block = order[n]
        arrived(twin_part.at[block], twin_recv.at[n])
        last_right, last_left = reach[plane][0] - 1, reach[plane][1] - 1
        arrived(right_part.at[plane, last_right], right_recv.at[plane, last_right])
        arrived(left_part.at[plane, last_left], left_recv.at[plane, last_left])
        extras = [(right_part, (plane, last_right)), (left_part, (plane, last_left))]
        if plane == 0:
            arrived(cross_part.at[0], cross_recv)
            extras.append((cross_part, (0,)))
        combine(block, extras)
        if plane == 1:
            send(part.at[block], cross_part.at[0], ring_send.at[n], cross_recv, cross, head)
            sent.append((block, ring_send.at[n]))

    final = order[-1]
    my_cols = pl.ds(pl.multiple_of(head * WIDTH, WIDTH), WIDTH)

    def send_pieces(step, _):
        peer = (head + step) % heads
        for side, dst in enumerate((dk_out, dv_out)):
            send(part.at[final, side, peer], dst.at[:, my_cols], piece_send, piece_recv.at[side], ctx, peer)
        return 0

    lax.fori_loop(1, heads, send_pieces, 0)
    for side, dst in enumerate((dk_out, dv_out)):
        copy = pltpu.make_async_copy(part.at[final, side, head], dst.at[:, my_cols], local_sem.at[3 + side])
        copy.start()
        own.append(copy)

    for copy in own:
        copy.wait()
    for block, sem in sent:
        arrived(part.at[block], sem)
    arrived(part.at[pl.ds(0, 2 * z_size)], twin_send)
    for which, dst in enumerate((o_out, dq_out)):
        rows = dst.at[:, pl.ds(0, (group - 1) * wide)]
        arrived(rows, row_send.at[which])
        arrived(rows, row_recv.at[which])
    arrived(part.at[final, :, pl.ds(0, heads - 1)], piece_send)
    for side, dst in enumerate((dk_out, dv_out)):
        arrived(dst.at[:, pl.ds(0, (heads - 1) * WIDTH)], piece_recv.at[side])


def scatter(o, dq, dkv, z_size, heads):
    group, tokens, wide = o.shape
    far = z_size // 2
    rows = jax.ShapeDtypeStruct((tokens, group * wide), o.dtype)
    pieces = jax.ShapeDtypeStruct((tokens, heads * WIDTH), o.dtype)
    block = dkv.shape[2:]
    hbm = pl.BlockSpec(memory_space=pl.ANY)
    dma = pltpu.SemaphoreType.DMA
    return pl.pallas_call(
        functools.partial(scatter_kernel, z_size, heads),
        out_shape=(rows, rows, pieces, pieces),
        in_specs=[hbm] * 3,
        out_specs=(hbm,) * 4,
        scratch_shapes=[
            pltpu.VMEM((2 * z_size,) + block, dkv.dtype),
            pltpu.VMEM((2 * z_size,) + block, dkv.dtype),
            pltpu.VMEM((2, far) + block, dkv.dtype),
            pltpu.VMEM((2, far) + block, dkv.dtype),
            pltpu.VMEM((1,) + block, dkv.dtype),
            dma((2,)), dma((2,)), dma, dma((2,)), dma((4 * far - 2 + 1,)), dma((2, far)), dma((2, far)),
            dma, dma, dma((2 * z_size,)), dma((5,)),
        ],
        compiler_params=pltpu.CompilerParams(
            collective_id=1, has_side_effects=True, vmem_limit_bytes=32 * 1024 * 1024
        ),
        name="scatter",
    )(o, dq, dkv)


def per_device(heads, z_size, queries, keys, values, output_gradient, doc_lengths, span_of):
    q, do, kv = gather(queries, output_gradient, keys, values, z_size, heads)
    mine = lax.axis_index("ctx").astype(jnp.int32)
    first = mine - mine % 2
    rows = (UNITS, SPAN, UNIT_HEADS * WIDTH)
    o, dq, dkv = attention(
        q.reshape(rows), do.reshape(rows), kv.reshape(N_CTX, 2, SPAN, WIDTH),
        span_of, doc_lengths, jnp.stack([first, first + 1]),
    )
    dkv = dkv.reshape((N_CTX // 2, 2) + kv.shape[1:])
    return scatter(o.reshape(q.shape), dq.reshape(q.shape), dkv, z_size, heads)


def solution(mesh):
    shard = P(("ctx", "head"), None)
    return jax.shard_map(
        functools.partial(per_device, mesh.shape["head"], N_CTX // 4),
        mesh=mesh,
        in_specs=(shard, shard, shard, shard, P(), P()),
        out_specs=(shard, shard, shard, shard),
        check_vma=False,
    )
```

time: 1040 us -> 128 us (0.12)
  the two profiles are of different devices: /device:TPU:4 before, /device:TPU:2 now
where the time goes in v1:
time: 128 us; the launch traced here: 127 us
  Pallas kernels  119 us (93%)
  local copies, waits for them, and re-layouts  7.11 us (6%)
    pallas_call x1, Pallas kernels, gather(): pl.pallas_call(functools.partial(gather_kernel, z_size, heads), out_shape...  43.9 us
    pallas_call x1, Pallas kernels, attention(): pl.pallas_call(attention_kernel, out_shape=(rows, rows, blocks), in_specs...  40.3 us
    pallas_call x1, Pallas kernels, scatter(): pl.pallas_call(functools.partial(scatter_kernel, z_size, heads), out_shap...  34.3 us
    unnamed x10, local copies, waits for them, and re-layouts  7.11 us

profile of v1, /device:TPU:2, one launch (start us, length us, event | category | flops | bytes accessed | tf_op | source)
XLA Modules:
  0.0 126.9 jit_solution(15475253763024891413)
XLA Ops:
  0.6 0.6 pad_add_fusion.unit_ref
  1.2 43.9 %gather.1 = (bf16[16,32,512]{2,1,0:T(8,128)(2,1)}, bf16[16,32,512]{2,1,0:T(8,128)(2,1)}, bf16[32,2,8,32,128]{4,3,2,1,0:T(8,128)(2,1)}) custom-call(bf16[32,8192]{1,0:T(8,128)(2,1)} %q_in.1, bf16[32,8192]{1,0:T(8,128)(2,1)} %do_in.1, bf16[32,1024]{1,0:T(8,128)(2,1)} %k_in.1, bf16[32,1024]{1,0:T(8,128)(2,1)} %v_in.1), custom_call_target="tpu_custom_call" | custom-call | tf_op jit(solution)/shard_map/gather/pallas_call | solution.py:368
  45.1 40.3 %attention.1 = (bf16[2,256,512]{2,1,0:T(8,128)(2,1)}, bf16[2,256,512]{2,1,0:T(8,128)(2,1)}, bf16[32,2,256,128]{3,2,1,0:T(8,128)(2,1)}) custom-call(s32[32]{0:T(128)} %span_ref.1, s32[4]{0:T(128)} %len_ref.1, s32[2]{0:T(128)} %pad_add_fusion.unit_ref, bf16[2,256,512]{2,1,0:T(8,128)(2,1)} %bitcast.12, bf16[2,256,512]{2,1,0:T(8,128)(2,1)} %bitcast.13, ...), custom_call_target="tpu_custom_call" | custom-call | tf_op jit(solution)/shard_map/attention/pallas_call | solution.py:182
  85.5 0.0 copy-start
  85.5 2.2 %copy-done = bf16[32,2,256,128]{3,2,1,0:T(8,128)(2,1)S(1)} copy-done((bf16[32,2,256,128]{3,2,1,0:T(8,128)(2,1)S(1)}, bf16[32,2,256,128]{3,2,1,0:T(8,128)(2,1)}, u32[]{:S(2)}) %copy-start) | copy-done | bytes 4194328
  87.6 0.0 copy-start.1
  87.7 1.0 copy-done.1
  88.7 0.0 copy-start.2
  88.7 1.0 copy-done.2
  89.7 34.3 %scatter.1 = (bf16[32,8192]{1,0:T(8,128)(2,1)S(1)}, bf16[32,8192]{1,0:T(8,128)(2,1)S(1)}, bf16[32,1024]{1,0:T(8,128)(2,1)S(1)}, bf16[32,1024]{1,0:T(8,128)(2,1)S(1)}) custom-call(bf16[16,32,512]{2,1,0:T(8,128)(2,1)S(1)} %bitcast.9, bf16[16,32,512]{2,1,0:T(8,128)(2,1)S(1)} %bitcast.10, bf16[16,2,2,8,32,128]{5,4,3,2,1,0:T(8,128)(2,1)S(1)} %bitcast.8), custom_call_target="tpu_custom_call" | custom-call | tf_op jit(solution)/shard_map/scatter/pallas_call | solution.py:524
  124.0 0.8 copy.14
  124.8 0.8 copy.15
  125.6 0.6 copy.16
  126.2 0.6 copy.17
Async XLA Ops:
  85.5 2.2 %copy-start = (bf16[32,2,256,128]{3,2,1,0:T(8,128)(2,1)S(1)}, bf16[32,2,256,128]{3,2,1,0:T(8,128)(2,1)}, u32[]{:S(2)}) copy-start(bf16[32,2,256,128]{3,2,1,0:T(8,128)(2,1)} %get-tuple-element.15) | copy-start | bytes 12582916
  87.6 1.0 copy-start.1
  88.7 1.0 copy-start.2

commit v2 on v1

--- a/solution.py
+++ b/solution.py
@@ -13,17 +13,19 @@
 WIDTH = 128
 UNIT_HEADS = 4
 UNITS = 2
-MAX_BLOCKS = 17
+MAX_BLOCKS = 18
+COLS = UNIT_HEADS * SPAN
+LIMIT = 2.0**60
 SCALE = WIDTH**-0.5
 LOG2_SCALE = SCALE * math.log2(math.e)
 NEG = -1e30
 
 
 def attention_kernel(
-    span_ref, len_ref, unit_ref, q_hbm, do_hbm, kv_hbm,
+    span_ref, len_ref, q_hbm, do_hbm, kv_hbm,
     o_hbm, dq_hbm, dkv_hbm,
-    holder, q_v, do_v, kv_v, o_v, dq_v, acc, dkv_v, scores, probs,
-    q_t, do_t, do_s, o_t, dq_t, top, total, sem, out_sem,
+    holder, q_v, do_v, kv_v, o_v, dq_v, acc, dkv_v, probs, grads,
+    q_t, do_t, q_s, do_s, o_t, dq_t, top, total, sem, out_sem,
 ):
     load_q = pltpu.make_async_copy(q_hbm, q_v, sem.at[0])
     load_do = pltpu.make_async_copy(do_hbm, do_v, sem.at[1])
@@ -31,6 +33,8 @@
     load_q.start()
     load_kv.start()
     load_do.start()
+    ctx = lax.axis_index("ctx")
+    first_unit = ctx - ctx % UNITS
 
     def note(c, _):
         holder[span_ref[c]] = c
@@ -59,97 +63,141 @@
             start = jnp.where(pos >= end, end, start)
         return start
 
+    def rows_of(i, count=1):
+        return pl.ds(pl.multiple_of(i * SPAN, SPAN), count * SPAN)
+
+    def cols_of(h):
+        return pl.ds(h * SPAN, SPAN)
+
     def unit(u, _):
-        span = span_ref[unit_ref[u]]
+        span = span_ref[first_unit + u]
         first_pos = span * SPAN
         first_block = doc_start(first_pos) // SPAN
         last_start = doc_start(first_pos + (SPAN - 1))
         blocks = span - first_block + 1
+        edges = jnp.maximum(jnp.minimum((last_start + (SPAN - 1)) // SPAN, span) - first_block, 0)
         q_pos = first_pos + lax.broadcasted_iota(jnp.int32, (1, SPAN), 1)
         q_start = doc_start(q_pos)
 
         for h in range(UNIT_HEADS):
-            cols = pl.ds(h * WIDTH, WIDTH)
-            q_t[h] = q_v[u, :, cols].T
-            do_t[h] = do_v[u, :, cols].T
-            top[h] = jnp.full((8, SPAN), NEG, jnp.float32)
-            total[h] = jnp.zeros((8, SPAN), jnp.float32)
-            o_t[h] = jnp.zeros((WIDTH, SPAN), jnp.float32)
-            dq_t[h] = jnp.zeros((WIDTH, SPAN), jnp.float32)
-
-        def score_block(i, masked):
-            t = first_block + i
-            k = kv_v[holder[t], 0]
+            lanes = pl.ds(h * WIDTH, WIDTH)
+            q_h = q_v[u, :, lanes]
+            q_s[cols_of(h)] = q_h
+            q_t[h] = q_h.T
+            do_t[h] = do_v[u, :, lanes].T
+
+        def clear_totals():
+            total[...] = jnp.zeros_like(total)
+            o_t[...] = jnp.zeros_like(o_t)
+
+        def allowed_at(t):
+            k_pos = t * SPAN + lax.broadcasted_iota(jnp.int32, (SPAN, SPAN), 0)
+            return (k_pos <= q_pos) & (k_pos >= q_start)
+
+        def fold(x, reduce):
+            return reduce(x.reshape(x.shape[0] // 8, 8, SPAN), axis=0)
+
+        def forward(i, count, masked, take_top=False):
+            places = [holder[first_block + i + n] for n in range(count)]
+            k = jnp.concatenate([kv_v[c, 0] for c in places], axis=0)
+            v_t = jnp.concatenate([kv_v[c, 1] for c in places], axis=0).T
             if masked:
-                k_pos = t * SPAN + lax.broadcasted_iota(jnp.int32, (SPAN, SPAN), 0)
-                allowed = (k_pos <= q_pos) & (k_pos >= q_start)
+                allowed = allowed_at(first_block + i)
             for h in range(UNIT_HEADS):
                 s = jnp.dot(k, q_t[h], preferred_element_type=jnp.float32)
                 if masked:
                     s = jnp.where(allowed, s, NEG)
-                scores[i, h] = s
-                top[h] = jnp.maximum(top[h], jnp.max(s.reshape(SPAN // 8, 8, SPAN), axis=0))
-
-        def score_step(i, _):
-            t = first_block + i
-            edge = (t == span) | (t * SPAN < last_start)
-
-            @pl.when(edge)
-            def _():
-                score_block(i, True)
-
-            @pl.when(jnp.logical_not(edge))
-            def _():
-                score_block(i, False)
-
+                if take_top:
+                    level = jnp.max(fold(s, jnp.max), axis=0, keepdims=True)
+                    top[h] = jnp.broadcast_to(level, (8, SPAN))
+                else:
+                    level = top[h, 0:1]
+                p = jnp.exp2((s - level) * LOG2_SCALE)
+                total[h] += fold(p, jnp.sum)
+                p = p.astype(jnp.bfloat16)
+                probs[rows_of(i, count), cols_of(h)] = p
+                o_t[h] += jnp.dot(v_t, p, preferred_element_type=jnp.float32)
+
+        def masked_step(i, _):
+            forward(i, 1, True)
             return 0
 
-        lax.fori_loop(0, blocks, score_step, 0)
+        clear_totals()
+        forward(blocks - 1, 1, True, take_top=True)
+        lax.fori_loop(0, edges, masked_step, 0)
+        inner = blocks - 1 - edges
+
+        def pair_step(j, _):
+            forward(edges + 2 * j, 2, False)
+            return 0
+
+        lax.fori_loop(0, inner // 2, pair_step, 0)
+
+        @pl.when(inner % 2 == 1)
+        def _():
+            forward(blocks - 2, 1, False)
+
+        worst = jnp.max(jnp.where(total[...] < LIMIT, 0.0, 1.0))
+
+        @pl.when(worst > 0.0)
+        def _():
+            clear_totals()
+            top[...] = jnp.full_like(top, NEG)
+
+            def top_step(i, _):
+                k = kv_v[holder[first_block + i], 0]
+                allowed = allowed_at(first_block + i)
+                for h in range(UNIT_HEADS):
+                    s = jnp.dot(k, q_t[h], preferred_element_type=jnp.float32)
+                    top[h] = jnp.maximum(top[h], fold(jnp.where(allowed, s, NEG), jnp.max))
+                return 0
+
+            lax.fori_loop(0, blocks, top_step, 0)
+            for h in range(UNIT_HEADS):
+                top[h] = jnp.broadcast_to(jnp.max(top[h], axis=0, keepdims=True), (8, SPAN))
+            lax.fori_loop(0, blocks, masked_step, 0)
+
         for h in range(UNIT_HEADS):
-            top[h] = jnp.broadcast_to(jnp.max(top[h], axis=0, keepdims=True), (8, SPAN))
-
-        def weight_step(i, _):
-            v_t = kv_v[holder[first_block + i], 1].T
-            for h in range(UNIT_HEADS):
-                p = jnp.exp2((scores[i, h] - top[h, 0:1]) * LOG2_SCALE)
-                total[h] += jnp.sum(p.reshape(SPAN // 8, 8, SPAN), axis=0)
-                p = p.astype(jnp.bfloat16)
-                probs[i, h] = p
-                o_t[h] += jnp.dot(v_t, p, preferred_element_type=jnp.float32)
-            return 0
-
-        lax.fori_loop(0, blocks, weight_step, 0)
-
-        for h in range(UNIT_HEADS):
-            cols = pl.ds(h * WIDTH, WIDTH)
+            lanes = pl.ds(h * WIDTH, WIDTH)
             inverse = 1.0 / jnp.sum(total[h], axis=0, keepdims=True)
             out = (o_t[h] * inverse).astype(jnp.bfloat16)
-            o_v[u, :, cols] = out.T
+            o_v[u, :, lanes] = out.T
             scaled = (do_t[h].astype(jnp.float32) * inverse).astype(jnp.bfloat16)
             do_t[h] = scaled
-            do_s[h] = scaled.T
+            do_s[cols_of(h)] = scaled.T
             delta = jnp.sum(scaled.astype(jnp.float32) * out.astype(jnp.float32), axis=0, keepdims=True)
             total[h] = jnp.broadcast_to(delta, (8, SPAN))
-
-        def grad_step(i, _):
-            c = holder[first_block + i]
-            k = kv_v[c, 0]
-            v = kv_v[c, 1]
-            k_t = k.T
-            dk = jnp.zeros((SPAN, WIDTH), jnp.float32)
-            dv = jnp.zeros((SPAN, WIDTH), jnp.float32)
+        dq_t[...] = jnp.zeros_like(dq_t)
+
+        def backward(i, count):
+            rows = rows_of(i, count)
+            here = pl.ds(0, count * SPAN)
+            places = [holder[first_block + i + n] for n in range(count)]
+            k_t = jnp.concatenate([kv_v[c, 0] for c in places], axis=0).T
+            v = jnp.concatenate([kv_v[c, 1] for c in places], axis=0)
             for h in range(UNIT_HEADS):
-                p = probs[i, h]
                 dp = jnp.dot(v, do_t[h], preferred_element_type=jnp.float32)
-                dv += jnp.dot(p, do_s[h], preferred_element_type=jnp.float32)
-                ds = (p.astype(jnp.float32) * (dp - total[h, 0:1])).astype(jnp.bfloat16)
-                dk += jnp.dot(ds, q_v[u, :, pl.ds(h * WIDTH, WIDTH)], preferred_element_type=jnp.float32)
+                p = probs[rows, cols_of(h)].astype(jnp.float32)
+                ds = (p * (dp - total[h, 0:1])).astype(jnp.bfloat16)
+                grads[here, cols_of(h)] = ds
                 dq_t[h] += jnp.dot(k_t, ds, preferred_element_type=jnp.float32)
-            acc[c, 0] += dk * SCALE
-            acc[c, 1] += dv
+            dv = jnp.dot(probs[rows], do_s[...], preferred_element_type=jnp.float32)
+            dk = jnp.dot(grads[here], q_s[...], preferred_element_type=jnp.float32)
+            for n, c in enumerate(places):
+                part = slice(n * SPAN, (n + 1) * SPAN)
+                acc[c, 0] += dk[part]
+                acc[c, 1] += dv[part]
+
+        def grad_step(j, _):
+            backward(2 * j, 2)
             return 0
 
-        lax.fori_loop(0, blocks, grad_step, 0)
+        lax.fori_loop(0, blocks // 2, grad_step, 0)
+
+        @pl.when(blocks % 2 == 1)
+        def _():
+            backward(blocks - 1, 1)
+
         for h in range(UNIT_HEADS):
             dq_v[u, :, pl.ds(h * WIDTH, WIDTH)] = (dq_t[h] * SCALE).astype(jnp.bfloat16).T
         return 0
@@ -161,18 +209,18 @@
     save_dq.start()
 
     def pack(c, _):
-        dkv_v[c] = acc[c].astype(jnp.bfloat16)
+        dkv_v[c, 0] = (acc[c, 0] * SCALE).astype(jnp.bfloat16)
+        dkv_v[c, 1] = acc[c, 1].astype(jnp.bfloat16)
+        pltpu.make_async_copy(dkv_v.at[c], dkv_hbm.at[c], out_sem.at[2]).start()
         return 0
 
     lax.fori_loop(0, N_CTX, pack, 0)
-    save_dkv = pltpu.make_async_copy(dkv_v, dkv_hbm, out_sem.at[2])
-    save_dkv.start()
     save_o.wait()
     save_dq.wait()
-    save_dkv.wait()
-
-
-def attention(q, do, kv, span_of, doc_lengths, unit_ctx):
+    pltpu.make_async_copy(dkv_v, dkv_hbm, out_sem.at[2]).wait()
+
+
+def attention(q, do, kv, span_of, doc_lengths):
     rows = jax.ShapeDtypeStruct((UNITS, SPAN, UNIT_HEADS * WIDTH), jnp.bfloat16)
     blocks = jax.ShapeDtypeStruct((N_CTX, 2, SPAN, WIDTH), jnp.bfloat16)
     smem = pl.BlockSpec(memory_space=pltpu.SMEM)
@@ -182,7 +230,7 @@
     return pl.pallas_call(
         attention_kernel,
         out_shape=(rows, rows, blocks),
-        in_specs=[smem, smem, smem, hbm, hbm, hbm],
+        in_specs=[smem, smem, hbm, hbm, hbm],
         out_specs=(hbm, hbm, hbm),
         scratch_shapes=[
             pltpu.SMEM((N_CTX,), jnp.int32),
@@ -193,11 +241,12 @@
             vmem(rows.shape, jnp.bfloat16),
             vmem(blocks.shape, jnp.float32),
             vmem(blocks.shape, jnp.bfloat16),
-            vmem((MAX_BLOCKS, UNIT_HEADS, SPAN, SPAN), jnp.float32),
-            vmem((MAX_BLOCKS, UNIT_HEADS, SPAN, SPAN), jnp.bfloat16),
+            vmem((MAX_BLOCKS * SPAN, COLS), jnp.bfloat16),
+            vmem((2 * SPAN, COLS), jnp.bfloat16),
             vmem(head_t, jnp.bfloat16),
             vmem(head_t, jnp.bfloat16),
-            vmem((UNIT_HEADS, SPAN, WIDTH), jnp.bfloat16),
+            vmem((COLS, WIDTH), jnp.bfloat16),
+            vmem((COLS, WIDTH), jnp.bfloat16),
             vmem(head_t, jnp.float32),
             vmem(head_t, jnp.float32),
             vmem((UNIT_HEADS, 8, SPAN), jnp.float32),
@@ -207,7 +256,7 @@
         ],
         compiler_params=pltpu.CompilerParams(vmem_limit_bytes=60 * 1024 * 1024),
         name="attention",
-    )(span_of, doc_lengths, unit_ctx, q, do, kv)
+    )(span_of, doc_lengths, q, do, kv)
 
 
 MESH_IDS = pl.DeviceIdType.MESH
@@ -374,7 +423,7 @@
             dma((2,)), dma((2,)), dma, dma, dma((4 * far - 2 + 1,)), dma((2, far)), dma((2, far)),
             dma, dma, dma, dma((4,)),
         ],
-        compiler_params=pltpu.CompilerParams(collective_id=0, has_side_effects=True),
+        compiler_params=pltpu.CompilerParams(collective_id=0, has_side_effects=True, vmem_limit_bytes=60 * 1024 * 1024),
         name="gather",
     )(q, do, k, v)
 
@@ -536,23 +585,43 @@
             dma, dma, dma((2 * z_size,)), dma((5,)),
         ],
         compiler_params=pltpu.CompilerParams(
-            collective_id=1, has_side_effects=True, vmem_limit_bytes=32 * 1024 * 1024
+            collective_id=1, has_side_effects=True, vmem_limit_bytes=60 * 1024 * 1024
         ),
         name="scatter",
     )(o, dq, dkv)
 
 
+def settle_kernel(*refs):
+    count = len(refs) // 2
+    sem = refs[-1]
+    copies = [pltpu.make_async_copy(refs[i], refs[count + i], sem.at[i]) for i in range(count)]
+    for copy in copies:
+        copy.start()
+    for copy in copies:
+        copy.wait()
+
+
+def settle(arrays):
+    hbm = pl.BlockSpec(memory_space=pl.ANY)
+    return pl.pallas_call(
+        settle_kernel,
+        out_shape=tuple(jax.ShapeDtypeStruct(a.shape, a.dtype) for a in arrays),
+        in_specs=[hbm] * len(arrays),
+        out_specs=(hbm,) * len(arrays),
+        scratch_shapes=[pltpu.SemaphoreType.DMA((len(arrays),))],
+        compiler_params=pltpu.CompilerParams(vmem_limit_bytes=60 * 1024 * 1024),
+        name="settle",
+    )(*arrays)
+
+
 def per_device(heads, z_size, queries, keys, values, output_gradient, doc_lengths, span_of):
     q, do, kv = gather(queries, output_gradient, keys, values, z_size, heads)
-    mine = lax.axis_index("ctx").astype(jnp.int32)
-    first = mine - mine % 2
     rows = (UNITS, SPAN, UNIT_HEADS * WIDTH)
     o, dq, dkv = attention(
-        q.reshape(rows), do.reshape(rows), kv.reshape(N_CTX, 2, SPAN, WIDTH),
-        span_of, doc_lengths, jnp.stack([first, first + 1]),
+        q.reshape(rows), do.reshape(rows), kv.reshape(N_CTX, 2, SPAN, WIDTH), span_of, doc_lengths
     )
     dkv = dkv.reshape((N_CTX // 2, 2) + kv.shape[1:])
-    return scatter(o.reshape(q.shape), dq.reshape(q.shape), dkv, z_size, heads)
+    return settle(scatter(o.reshape(q.shape), dq.reshape(q.shape), dkv, z_size, heads))
 
 
 def solution(mesh):

time: 128 us -> 183 us (1.43)
  Pallas kernels: 119 us -> 181 us
  local copies, waits for them, and re-layouts: 7.11 us -> 0 us
    pallas_call x0 -> x1, Pallas kernels: none -> 36.9 us  [settle(): pl.pallas_call(settle_kernel, out_shape=tuple((jax.ShapeDtypeStruct(a.sha...]
    pallas_call x1, Pallas kernels: 34.3 us -> 70.9 us  [scatter(): pl.pallas_call(functools.partial(scatter_kernel, z_size, heads), out_shap...]
    pallas_call x1, Pallas kernels: 40.3 us -> 29.2 us  [attention(): pl.pallas_call(attention_kernel, out_shape=(rows, rows, blocks), in_specs...]
    unnamed x10 -> x0, local copies, waits for them, and re-layouts: 7.11 us -> none
where the time goes in v2:
time: 183 us; the launch traced here: 182 us
  Pallas kernels  181 us (99%)
    pallas_call x1, Pallas kernels, scatter(): pl.pallas_call(functools.partial(scatter_kernel, z_size, heads), out_shap...  70.9 us
    pallas_call x1, Pallas kernels, gather(): pl.pallas_call(functools.partial(gather_kernel, z_size, heads), out_shape...  44.3 us
    pallas_call x1, Pallas kernels, settle(): pl.pallas_call(settle_kernel, out_shape=tuple((jax.ShapeDtypeStruct(a.sha...  36.9 us
    pallas_call x1, Pallas kernels, attention(): pl.pallas_call(attention_kernel, out_shape=(rows, rows, blocks), in_specs...  29.2 us

profile of v2, /device:TPU:2, one launch (start us, length us, event | category | flops | bytes accessed | tf_op | source)
XLA Modules:
  0.0 181.9 jit_solution(4119276221707481410)
XLA Ops:
  0.6 44.3 %gather.1 = (bf16[16,32,512]{2,1,0:T(8,128)(2,1)}, bf16[16,32,512]{2,1,0:T(8,128)(2,1)}, bf16[32,2,8,32,128]{4,3,2,1,0:T(8,128)(2,1)}) custom-call(bf16[32,8192]{1,0:T(8,128)(2,1)} %q_in.1, bf16[32,8192]{1,0:T(8,128)(2,1)} %do_in.1, bf16[32,1024]{1,0:T(8,128)(2,1)} %k_in.1, bf16[32,1024]{1,0:T(8,128)(2,1)} %v_in.1), custom_call_target="tpu_custom_call" | custom-call | tf_op jit(solution)/shard_map/gather/pallas_call | solution.py:417
  44.9 29.2 %attention.1 = (bf16[2,256,512]{2,1,0:T(8,128)(2,1)}, bf16[2,256,512]{2,1,0:T(8,128)(2,1)}, bf16[32,2,256,128]{3,2,1,0:T(8,128)(2,1)}) custom-call(s32[32]{0:T(128)} %span_ref.1, s32[4]{0:T(128)} %len_ref.1, bf16[2,256,512]{2,1,0:T(8,128)(2,1)} %bitcast.10, bf16[2,256,512]{2,1,0:T(8,128)(2,1)} %bitcast.11, bf16[32,2,256,128]{3,2,1,0:T(8,128)(2,1)} %bitcast.7), custom_call_target="tpu_custom_call" | custom-call | tf_op jit(solution)/shard_map/attention/pallas_call | solution.py:230
  74.2 70.9 %scatter.1 = (bf16[32,8192]{1,0:T(8,128)(2,1)}, bf16[32,8192]{1,0:T(8,128)(2,1)}, bf16[32,1024]{1,0:T(8,128)(2,1)}, bf16[32,1024]{1,0:T(8,128)(2,1)}) custom-call(bf16[16,32,512]{2,1,0:T(8,128)(2,1)} %bitcast.8, bf16[16,32,512]{2,1,0:T(8,128)(2,1)} %bitcast.9, bf16[16,2,2,8,32,128]{5,4,3,2,1,0:T(8,128)(2,1)} %bitcast.6), custom_call_target="tpu_custom_call" | custom-call | tf_op jit(solution)/shard_map/scatter/pallas_call | solution.py:573
  145.1 36.9 %settle.1 = (bf16[32,8192]{1,0:T(8,128)(2,1)}, bf16[32,8192]{1,0:T(8,128)(2,1)}, bf16[32,1024]{1,0:T(8,128)(2,1)}, bf16[32,1024]{1,0:T(8,128)(2,1)}) custom-call(bf16[32,8192]{1,0:T(8,128)(2,1)} %get-tuple-element.20.refs_0_, bf16[32,8192]{1,0:T(8,128)(2,1)} %get-tuple-element.21.refs_1_, bf16[32,1024]{1,0:T(8,128)(2,1)} %get-tuple-element.22.refs_2_, ...), custom_call_target="tpu_custom_call" | custom-call | tf_op jit(solution)/shard_map/settle/pallas_call | solution.py:606

commit v3 on v2

--- a/solution.py
+++ b/solution.py
@@ -21,18 +21,15 @@
 NEG = -1e30
 
 
+NT = (((1,), (1,)), ((), ()))
+
+
 def attention_kernel(
-    span_ref, len_ref, q_hbm, do_hbm, kv_hbm,
-    o_hbm, dq_hbm, dkv_hbm,
-    holder, q_v, do_v, kv_v, o_v, dq_v, acc, dkv_v, probs, grads,
-    q_t, do_t, q_s, do_s, o_t, dq_t, top, total, sem, out_sem,
+    span_ref, len_ref, q_v, do_v, kv_v,
+    o_v, dq_v, dkv_v,
+    holder, acc, probs, grads, wide_buf,
+    q_t, do_t, q_s, do_s, o_acc, dq_acc, level_b, delta_b, starts,
 ):
-    load_q = pltpu.make_async_copy(q_hbm, q_v, sem.at[0])
-    load_do = pltpu.make_async_copy(do_hbm, do_v, sem.at[1])
-    load_kv = pltpu.make_async_copy(kv_hbm, kv_v, sem.at[2])
-    load_q.start()
-    load_kv.start()
-    load_do.start()
     ctx = lax.axis_index("ctx")
     first_unit = ctx - ctx % UNITS
 
@@ -43,13 +40,10 @@
     lax.fori_loop(0, N_CTX, note, 0)
 
     def clear(c, _):
-        acc[c] = jnp.zeros((2, SPAN, WIDTH), jnp.float32)
+        acc[c] = jnp.zeros((2, WIDTH, SPAN), jnp.float32)
         return 0
 
     lax.fori_loop(0, N_CTX, clear, 0)
-    load_q.wait()
-    load_do.wait()
-    load_kv.wait()
 
     ends = []
     running = jnp.int32(0)
@@ -63,11 +57,22 @@
             start = jnp.where(pos >= end, end, start)
         return start
 
-    def rows_of(i, count=1):
-        return pl.ds(pl.multiple_of(i * SPAN, SPAN), count * SPAN)
-
-    def cols_of(h):
+    def rows_of(h):
         return pl.ds(h * SPAN, SPAN)
+
+    def lanes_of(h):
+        return pl.ds(h * WIDTH, WIDTH)
+
+    def both(x):
+        return jnp.concatenate([x, x], axis=1)
+
+    def beside(parts):
+        return parts[0] if len(parts) == 1 else jnp.concatenate(parts, axis=1)
+
+    def below(parts):
+        return parts[0] if len(parts) == 1 else jnp.concatenate(parts, axis=0)
+
+    ones = jnp.ones((SPAN, WIDTH), jnp.bfloat16)
 
     def unit(u, _):
         span = span_ref[first_unit + u]
@@ -76,53 +81,54 @@
         last_start = doc_start(first_pos + (SPAN - 1))
         blocks = span - first_block + 1
         edges = jnp.maximum(jnp.minimum((last_start + (SPAN - 1)) // SPAN, span) - first_block, 0)
-        q_pos = first_pos + lax.broadcasted_iota(jnp.int32, (1, SPAN), 1)
-        q_start = doc_start(q_pos)
+        starts[...] = doc_start(first_pos + lax.broadcasted_iota(jnp.int32, (SPAN, WIDTH), 0))
 
         for h in range(UNIT_HEADS):
-            lanes = pl.ds(h * WIDTH, WIDTH)
-            q_h = q_v[u, :, lanes]
-            q_s[cols_of(h)] = q_h
-            q_t[h] = q_h.T
-            do_t[h] = do_v[u, :, lanes].T
-
-        def clear_totals():
-            total[...] = jnp.zeros_like(total)
-            o_t[...] = jnp.zeros_like(o_t)
+            q_h = q_v[u, :, lanes_of(h)]
+            q_s[rows_of(h)] = q_h
+            q_t[:, rows_of(h)] = q_h.T
 
         def allowed_at(t):
-            k_pos = t * SPAN + lax.broadcasted_iota(jnp.int32, (SPAN, SPAN), 0)
-            return (k_pos <= q_pos) & (k_pos >= q_start)
-
-        def fold(x, reduce):
-            return reduce(x.reshape(x.shape[0] // 8, 8, SPAN), axis=0)
+            k_pos = t * SPAN + lax.broadcasted_iota(jnp.int32, (SPAN, SPAN), 1)
+            q_pos = first_pos + lax.broadcasted_iota(jnp.int32, (SPAN, SPAN), 0)
+            return (k_pos <= q_pos) & (k_pos >= both(starts[...]))
+
+        def halves_max(s):
+            return jnp.maximum(s[:, :WIDTH], s[:, WIDTH:])
+
+        def row_max(x):
+            return jnp.broadcast_to(jnp.max(x, axis=1, keepdims=True), x.shape)
 
         def forward(i, count, masked, take_top=False):
             places = [holder[first_block + i + n] for n in range(count)]
-            k = jnp.concatenate([kv_v[c, 0] for c in places], axis=0)
-            v_t = jnp.concatenate([kv_v[c, 1] for c in places], axis=0).T
+            for n, c in enumerate(places):
+                wide_buf[n] = lax.dot_general(
+                    q_s[...], kv_v[c, 0], NT, preferred_element_type=jnp.float32
+                )
             if masked:
                 allowed = allowed_at(first_block + i)
-            for h in range(UNIT_HEADS):
-                s = jnp.dot(k, q_t[h], preferred_element_type=jnp.float32)
-                if masked:
-                    s = jnp.where(allowed, s, NEG)
-                if take_top:
-                    level = jnp.max(fold(s, jnp.max), axis=0, keepdims=True)
-                    top[h] = jnp.broadcast_to(level, (8, SPAN))
-                else:
-                    level = top[h, 0:1]
-                p = jnp.exp2((s - level) * LOG2_SCALE)
-                total[h] += fold(p, jnp.sum)
-                p = p.astype(jnp.bfloat16)
-                probs[rows_of(i, count), cols_of(h)] = p
-                o_t[h] += jnp.dot(v_t, p, preferred_element_type=jnp.float32)
+            for n in range(count):
+                for h in range(UNIT_HEADS):
+                    s = wide_buf[n, rows_of(h)]
+                    if masked:
+                        s = jnp.where(allowed, s, NEG)
+                    if take_top:
+                        level = row_max(halves_max(s))
+                        level_b[rows_of(h)] = level
+                    else:
+                        level = level_b[rows_of(h)]
+                    p = jnp.exp2((s - both(level)) * LOG2_SCALE)
+                    probs[i + n, rows_of(h)] = p.astype(jnp.bfloat16)
+            values = below([beside([kv_v[c, 1], ones]) for c in places])
+            o_acc[...] += jnp.dot(
+                beside([probs[i + n] for n in range(count)]), values, preferred_element_type=jnp.float32
+            )
 
         def masked_step(i, _):
             forward(i, 1, True)
             return 0
 
-        clear_totals()
+        o_acc[...] = jnp.zeros_like(o_acc)
         forward(blocks - 1, 1, True, take_top=True)
         lax.fori_loop(0, edges, masked_step, 0)
         inner = blocks - 1 - edges
@@ -137,56 +143,61 @@
         def _():
             forward(blocks - 2, 1, False)
 
-        worst = jnp.max(jnp.where(total[...] < LIMIT, 0.0, 1.0))
+        worst = jnp.max(jnp.where(o_acc[:, WIDTH:] < LIMIT, 0.0, 1.0))
 
         @pl.when(worst > 0.0)
         def _():
-            clear_totals()
-            top[...] = jnp.full_like(top, NEG)
+            o_acc[...] = jnp.zeros_like(o_acc)
+            level_b[...] = jnp.full_like(level_b, NEG)
 
             def top_step(i, _):
                 k = kv_v[holder[first_block + i], 0]
                 allowed = allowed_at(first_block + i)
                 for h in range(UNIT_HEADS):
-                    s = jnp.dot(k, q_t[h], preferred_element_type=jnp.float32)
-                    top[h] = jnp.maximum(top[h], fold(jnp.where(allowed, s, NEG), jnp.max))
+                    s = lax.dot_general(q_s[rows_of(h)], k, NT, preferred_element_type=jnp.float32)
+                    s = jnp.where(allowed, s, NEG)
+                    level_b[rows_of(h)] = jnp.maximum(level_b[rows_of(h)], halves_max(s))
                 return 0
 
             lax.fori_loop(0, blocks, top_step, 0)
             for h in range(UNIT_HEADS):
-                top[h] = jnp.broadcast_to(jnp.max(top[h], axis=0, keepdims=True), (8, SPAN))
+                level_b[rows_of(h)] = row_max(level_b[rows_of(h)])
             lax.fori_loop(0, blocks, masked_step, 0)
 
         for h in range(UNIT_HEADS):
-            lanes = pl.ds(h * WIDTH, WIDTH)
-            inverse = 1.0 / jnp.sum(total[h], axis=0, keepdims=True)
-            out = (o_t[h] * inverse).astype(jnp.bfloat16)
-            o_v[u, :, lanes] = out.T
-            scaled = (do_t[h].astype(jnp.float32) * inverse).astype(jnp.bfloat16)
-            do_t[h] = scaled
-            do_s[cols_of(h)] = scaled.T
-            delta = jnp.sum(scaled.astype(jnp.float32) * out.astype(jnp.float32), axis=0, keepdims=True)
-            total[h] = jnp.broadcast_to(delta, (8, SPAN))
-        dq_t[...] = jnp.zeros_like(dq_t)
+            inverse = 1.0 / o_acc[rows_of(h), WIDTH:]
+            out = (o_acc[rows_of(h), :WIDTH] * inverse).astype(jnp.bfloat16)
+            o_v[u, :, lanes_of(h)] = out
+            scaled = (do_v[u, :, lanes_of(h)].astype(jnp.float32) * inverse).astype(jnp.bfloat16)
+            do_s[rows_of(h)] = scaled
+            do_t[:, rows_of(h)] = scaled.T
+            delta = jnp.sum(scaled.astype(jnp.float32) * out.astype(jnp.float32), axis=1, keepdims=True)
+            delta_b[rows_of(h)] = jnp.broadcast_to(delta, (SPAN, WIDTH))
+        dq_acc[...] = jnp.zeros_like(dq_acc)
 
         def backward(i, count):
-            rows = rows_of(i, count)
-            here = pl.ds(0, count * SPAN)
             places = [holder[first_block + i + n] for n in range(count)]
-            k_t = jnp.concatenate([kv_v[c, 0] for c in places], axis=0).T
-            v = jnp.concatenate([kv_v[c, 1] for c in places], axis=0)
-            for h in range(UNIT_HEADS):
-                dp = jnp.dot(v, do_t[h], preferred_element_type=jnp.float32)
-                p = probs[rows, cols_of(h)].astype(jnp.float32)
-                ds = (p * (dp - total[h, 0:1])).astype(jnp.bfloat16)
-                grads[here, cols_of(h)] = ds
-                dq_t[h] += jnp.dot(k_t, ds, preferred_element_type=jnp.float32)
-            dv = jnp.dot(probs[rows], do_s[...], preferred_element_type=jnp.float32)
-            dk = jnp.dot(grads[here], q_s[...], preferred_element_type=jnp.float32)
+            for n, c in enumerate(places):
+                wide_buf[n] = lax.dot_general(
+                    do_s[...], kv_v[c, 1], NT, preferred_element_type=jnp.float32
+                )
+            for n in range(count):
+                for h in range(UNIT_HEADS):
+                    p = probs[i + n, rows_of(h)].astype(jnp.float32)
+                    ds = p * (wide_buf[n, rows_of(h)] - both(delta_b[rows_of(h)]))
+                    grads[n, rows_of(h)] = ds.astype(jnp.bfloat16)
+            dv = jnp.dot(
+                do_t[...], beside([probs[i + n] for n in range(count)]), preferred_element_type=jnp.float32
+            )
+            ds = beside([grads[n] for n in range(count)])
+            dk = jnp.dot(q_t[...], ds, preferred_element_type=jnp.float32)
+            dq_acc[...] += jnp.dot(
+                ds, below([kv_v[c, 0] for c in places]), preferred_element_type=jnp.float32
+            )
             for n, c in enumerate(places):
                 part = slice(n * SPAN, (n + 1) * SPAN)
-                acc[c, 0] += dk[part]
-                acc[c, 1] += dv[part]
+                acc[c, 0] += dk[:, part]
+                acc[c, 1] += dv[:, part]
 
         def grad_step(j, _):
             backward(2 * j, 2)
@@ -199,62 +210,47 @@
             backward(blocks - 1, 1)
 
         for h in range(UNIT_HEADS):
-            dq_v[u, :, pl.ds(h * WIDTH, WIDTH)] = (dq_t[h] * SCALE).astype(jnp.bfloat16).T
+            dq_v[u, :, lanes_of(h)] = (dq_acc[rows_of(h)] * SCALE).astype(jnp.bfloat16)
         return 0
 
     lax.fori_loop(0, UNITS, unit, 0)
-    save_o = pltpu.make_async_copy(o_v, o_hbm, out_sem.at[0])
-    save_dq = pltpu.make_async_copy(dq_v, dq_hbm, out_sem.at[1])
-    save_o.start()
-    save_dq.start()
 
     def pack(c, _):
         dkv_v[c, 0] = (acc[c, 0] * SCALE).astype(jnp.bfloat16)
         dkv_v[c, 1] = acc[c, 1].astype(jnp.bfloat16)
-        pltpu.make_async_copy(dkv_v.at[c], dkv_hbm.at[c], out_sem.at[2]).start()
         return 0
 
     lax.fori_loop(0, N_CTX, pack, 0)
-    save_o.wait()
-    save_dq.wait()
-    pltpu.make_async_copy(dkv_v, dkv_hbm, out_sem.at[2]).wait()
 
 
 def attention(q, do, kv, span_of, doc_lengths):
     rows = jax.ShapeDtypeStruct((UNITS, SPAN, UNIT_HEADS * WIDTH), jnp.bfloat16)
-    blocks = jax.ShapeDtypeStruct((N_CTX, 2, SPAN, WIDTH), jnp.bfloat16)
+    blocks = jax.ShapeDtypeStruct((N_CTX, 2, WIDTH, SPAN), jnp.bfloat16)
     smem = pl.BlockSpec(memory_space=pltpu.SMEM)
-    hbm = pl.BlockSpec(memory_space=pl.ANY)
+    here = pl.BlockSpec(memory_space=pltpu.VMEM)
     vmem = pltpu.VMEM
-    head_t = (UNIT_HEADS, WIDTH, SPAN)
     return pl.pallas_call(
         attention_kernel,
         out_shape=(rows, rows, blocks),
-        in_specs=[smem, smem, hbm, hbm, hbm],
-        out_specs=(hbm, hbm, hbm),
+        in_specs=[smem, smem, here, here, here],
+        out_specs=(here, here, here),
         scratch_shapes=[
             pltpu.SMEM((N_CTX,), jnp.int32),
-            vmem(rows.shape, jnp.bfloat16),
-            vmem(rows.shape, jnp.bfloat16),
-            vmem(blocks.shape, jnp.bfloat16),
-            vmem(rows.shape, jnp.bfloat16),
-            vmem(rows.shape, jnp.bfloat16),
             vmem(blocks.shape, jnp.float32),
-            vmem(blocks.shape, jnp.bfloat16),
-            vmem((MAX_BLOCKS * SPAN, COLS), jnp.bfloat16),
-            vmem((2 * SPAN, COLS), jnp.bfloat16),
-            vmem(head_t, jnp.bfloat16),
-            vmem(head_t, jnp.bfloat16),
+            vmem((MAX_BLOCKS, COLS, SPAN), jnp.bfloat16),
+            vmem((2, COLS, SPAN), jnp.bfloat16),
+            vmem((2, COLS, SPAN), jnp.float32),
+            vmem((WIDTH, COLS), jnp.bfloat16),
+            vmem((WIDTH, COLS), jnp.bfloat16),
             vmem((COLS, WIDTH), jnp.bfloat16),
             vmem((COLS, WIDTH), jnp.bfloat16),
-            vmem(head_t, jnp.float32),
-            vmem(head_t, jnp.float32),
-            vmem((UNIT_HEADS, 8, SPAN), jnp.float32),
-            vmem((UNIT_HEADS, 8, SPAN), jnp.float32),
-            pltpu.SemaphoreType.DMA((3,)),
-            pltpu.SemaphoreType.DMA((3,)),
+            vmem((COLS, 2 * WIDTH), jnp.float32),
+            vmem((COLS, WIDTH), jnp.float32),
+            vmem((COLS, WIDTH), jnp.float32),
+            vmem((COLS, WIDTH), jnp.float32),
+            vmem((SPAN, WIDTH), jnp.int32),
         ],
-        compiler_params=pltpu.CompilerParams(vmem_limit_bytes=60 * 1024 * 1024),
+        compiler_params=pltpu.CompilerParams(vmem_limit_bytes=40 * 1024 * 1024),
         name="attention",
     )(span_of, doc_lengths, q, do, kv)
 
@@ -297,10 +293,14 @@
 
 def gather_kernel(
     z_size, heads,
-    q_in, do_in, k_in, v_in, q_out, do_out, kv_out,
+    q_hbm, do_hbm, k_hbm, v_hbm, q_out, do_out, kv_out, q_in, do_in, k_in, v_in,
     row_send, row_recv, piece_send, piece_recv, ring_send, right_recv, left_recv,
-    cross_recv, twin_send, twin_recv, local_sem,
+    cross_recv, twin_send, twin_recv, local_sem, load_sem,
 ):
+    loads = []
+    for n, (src, dst) in enumerate(((k_hbm, k_in), (v_hbm, v_in), (q_hbm, q_in), (do_hbm, do_in))):
+        loads.append(pltpu.make_async_copy(src, dst, load_sem.at[n]))
+        loads[-1].start()
     ctx, head, x, z, core = place(z_size)
     group = 2 * heads
     base = ctx - core
@@ -330,6 +330,8 @@
             )
         return 0
 
+    loads[0].wait()
+    loads[1].wait()
     lax.fori_loop(1, heads, send_pieces, 0)
     own = []
     for side, ref in enumerate((k_in, v_in)):
@@ -352,6 +354,7 @@
         copy.start()
         own.append(copy)
 
+    loads[2].wait()
     send_rows(q_in, q_out, 0)
     own[0].wait()
     own[1].wait()
@@ -374,6 +377,7 @@
     forward(ctx, right, right_recv.at[0, 0])
     forward(ctx, left, left_recv.at[0, 0])
     share(ctx)
+    loads[3].wait()
     send_rows(do_in, do_out, 1)
     arrived(kv_out.at[cross], cross_recv)
     forward(cross, right, right_recv.at[1, 0])
@@ -413,17 +417,18 @@
     rows = jax.ShapeDtypeStruct((group, tokens, q.shape[1] // group), q.dtype)
     kv = jax.ShapeDtypeStruct((4 * z_size, 2, heads, tokens, WIDTH), q.dtype)
     hbm = pl.BlockSpec(memory_space=pl.ANY)
+    here = pl.BlockSpec(memory_space=pltpu.VMEM)
     dma = pltpu.SemaphoreType.DMA
     return pl.pallas_call(
         functools.partial(gather_kernel, z_size, heads),
         out_shape=(rows, rows, kv),
         in_specs=[hbm] * 4,
-        out_specs=(hbm, hbm, hbm),
-        scratch_shapes=[
+        out_specs=(here, here, here),
+        scratch_shapes=[pltpu.VMEM(a.shape, a.dtype) for a in (q, do, k, v)] + [
             dma((2,)), dma((2,)), dma, dma, dma((4 * far - 2 + 1,)), dma((2, far)), dma((2, far)),
-            dma, dma, dma, dma((4,)),
+            dma, dma, dma, dma((4,)), dma((4,)),
         ],
-        compiler_params=pltpu.CompilerParams(collective_id=0, has_side_effects=True, vmem_limit_bytes=60 * 1024 * 1024),
+        compiler_params=pltpu.CompilerParams(collective_id=0, has_side_effects=True, vmem_limit_bytes=58 * 1024 * 1024),
         name="gather",
     )(q, do, k, v)
 
@@ -431,7 +436,7 @@
 def scatter_kernel(
     z_size, heads,
     o_in, dq_in, dkv_in, o_out, dq_out, dk_out, dv_out,
-    part, twin_part, right_part, left_part, cross_part,
+    part, twin_part, right_part, left_part, cross_part, final,
     row_send, row_recv, piece_send, piece_recv, ring_send, right_recv, left_recv,
     cross_recv, twin_send, twin_recv, local_sem,
 ):
@@ -490,12 +495,15 @@
         copy.start()
         own.append(copy)
 
-    def combine(block, extras):
+    def combine(block, extras, last=False):
         def add_half(side, _):
             total = part[block, side].astype(jnp.float32) + twin_part[block, side].astype(jnp.float32)
             for ref, at in extras:
                 total = total + ref[at + (side,)].astype(jnp.float32)
-            part[block, side] = total.astype(part.dtype)
+            if last:
+                final[side] = total.T.astype(final.dtype).reshape(final.shape[1:])
+            else:
+                part[block, side] = total.astype(part.dtype)
             return 0
 
         lax.fori_loop(0, 2, add_half, 0)
@@ -528,23 +536,22 @@
         if plane == 0:
             arrived(cross_part.at[0], cross_recv)
             extras.append((cross_part, (0,)))
-        combine(block, extras)
+        combine(block, extras, last=plane == 0)
         if plane == 1:
             send(part.at[block], cross_part.at[0], ring_send.at[n], cross_recv, cross, head)
             sent.append((block, ring_send.at[n]))
 
-    final = order[-1]
     my_cols = pl.ds(pl.multiple_of(head * WIDTH, WIDTH), WIDTH)
 
     def send_pieces(step, _):
         peer = (head + step) % heads
         for side, dst in enumerate((dk_out, dv_out)):
-            send(part.at[final, side, peer], dst.at[:, my_cols], piece_send, piece_recv.at[side], ctx, peer)
+            send(final.at[side, peer], dst.at[:, my_cols], piece_send, piece_recv.at[side], ctx, peer)
         return 0
 
     lax.fori_loop(1, heads, send_pieces, 0)
     for side, dst in enumerate((dk_out, dv_out)):
-        copy = pltpu.make_async_copy(part.at[final, side, head], dst.at[:, my_cols], local_sem.at[3 + side])
+        copy = pltpu.make_async_copy(final.at[side, head], dst.at[:, my_cols], local_sem.at[3 + side])
         copy.start()
         own.append(copy)
 
@@ -557,7 +564,7 @@
         rows = dst.at[:, pl.ds(0, (group - 1) * wide)]
         arrived(rows, row_send.at[which])
         arrived(rows, row_recv.at[which])
-    arrived(part.at[final, :, pl.ds(0, heads - 1)], piece_send)
+    arrived(final.at[:, pl.ds(0, heads - 1)], piece_send)
     for side, dst in enumerate((dk_out, dv_out)):
         arrived(dst.at[:, pl.ds(0, (heads - 1) * WIDTH)], piece_recv.at[side])
 
@@ -568,24 +575,25 @@
     rows = jax.ShapeDtypeStruct((tokens, group * wide), o.dtype)
     pieces = jax.ShapeDtypeStruct((tokens, heads * WIDTH), o.dtype)
     block = dkv.shape[2:]
-    hbm = pl.BlockSpec(memory_space=pl.ANY)
+    here = pl.BlockSpec(memory_space=pltpu.VMEM)
     dma = pltpu.SemaphoreType.DMA
     return pl.pallas_call(
         functools.partial(scatter_kernel, z_size, heads),
         out_shape=(rows, rows, pieces, pieces),
-        in_specs=[hbm] * 3,
-        out_specs=(hbm,) * 4,
+        in_specs=[here] * 3,
+        out_specs=(here,) * 4,
         scratch_shapes=[
             pltpu.VMEM((2 * z_size,) + block, dkv.dtype),
             pltpu.VMEM((2 * z_size,) + block, dkv.dtype),
             pltpu.VMEM((2, far) + block, dkv.dtype),
             pltpu.VMEM((2, far) + block, dkv.dtype),
             pltpu.VMEM((1,) + block, dkv.dtype),
+            pltpu.VMEM((2, heads, tokens, WIDTH), dkv.dtype),
             dma((2,)), dma((2,)), dma, dma((2,)), dma((4 * far - 2 + 1,)), dma((2, far)), dma((2, far)),
             dma, dma, dma((2 * z_size,)), dma((5,)),
         ],
         compiler_params=pltpu.CompilerParams(
-            collective_id=1, has_side_effects=True, vmem_limit_bytes=60 * 1024 * 1024
+            collective_id=1, has_side_effects=True, vmem_limit_bytes=24 * 1024 * 1024
         ),
         name="scatter",
     )(o, dq, dkv)
@@ -603,13 +611,14 @@
 
 def settle(arrays):
     hbm = pl.BlockSpec(memory_space=pl.ANY)
+    here = pl.BlockSpec(memory_space=pltpu.VMEM)
     return pl.pallas_call(
         settle_kernel,
         out_shape=tuple(jax.ShapeDtypeStruct(a.shape, a.dtype) for a in arrays),
-        in_specs=[hbm] * len(arrays),
+        in_specs=[here] * len(arrays),
         out_specs=(hbm,) * len(arrays),
         scratch_shapes=[pltpu.SemaphoreType.DMA((len(arrays),))],
-        compiler_params=pltpu.CompilerParams(vmem_limit_bytes=60 * 1024 * 1024),
+        compiler_params=pltpu.CompilerParams(vmem_limit_bytes=32 * 1024 * 1024),
         name="settle",
     )(*arrays)
 
@@ -620,7 +629,7 @@
     o, dq, dkv = attention(
         q.reshape(rows), do.reshape(rows), kv.reshape(N_CTX, 2, SPAN, WIDTH), span_of, doc_lengths
     )
-    dkv = dkv.reshape((N_CTX // 2, 2) + kv.shape[1:])
+    dkv = dkv.reshape((N_CTX // 2, 2) + dkv.shape[1:])
     return settle(scatter(o.reshape(q.shape), dq.reshape(q.shape), dkv, z_size, heads))
 
 

time: 183 us -> 116 us (0.63)
  Pallas kernels: 181 us -> 110 us
  local copies, waits for them, and re-layouts: 0 us -> 5.57 us
    pallas_call x1, Pallas kernels: 36.9 us -> 1.03 us  [settle(): pl.pallas_call(settle_kernel, out_shape=tuple((jax.ShapeDtypeStruct(a.sha...]
    pallas_call x1, Pallas kernels: 70.9 us -> 51.5 us  [scatter(): pl.pallas_call(functools.partial(scatter_kernel, z_size, heads), out_shap...]
    pallas_call x1, Pallas kernels: 29.2 us -> 11.9 us  [attention(): pl.pallas_call(attention_kernel, out_shape=(rows, rows, blocks), in_specs...]
    unnamed x0 -> x10, local copies, waits for them, and re-layouts: none -> 5.57 us
where the time goes in v3:
time: 116 us
  Pallas kernels  110 us (95%)
  local copies, waits for them, and re-layouts  5.57 us (5%)
    pallas_call x1, Pallas kernels, scatter(): pl.pallas_call(functools.partial(scatter_kernel, z_size, heads), out_shap...  51.5 us
    pallas_call x1, Pallas kernels, gather(): pl.pallas_call(functools.partial(gather_kernel, z_size, heads), out_shape...  45.1 us
    pallas_call x1, Pallas kernels, attention(): pl.pallas_call(attention_kernel, out_shape=(rows, rows, blocks), in_specs...  11.9 us
    unnamed x10, local copies, waits for them, and re-layouts  5.57 us

profile of v3, /device:TPU:2, one launch (start us, length us, event | category | flops | bytes accessed | tf_op | source)
XLA Modules:
  0.0 115.9 jit_solution(8490261640536942373)
XLA Ops:
  0.6 45.1 %gather.1 = (bf16[16,32,512]{2,1,0:T(8,128)(2,1)}, bf16[16,32,512]{2,1,0:T(8,128)(2,1)}, bf16[32,2,8,32,128]{4,3,2,1,0:T(8,128)(2,1)}) custom-call(bf16[32,8192]{1,0:T(8,128)(2,1)} %q_hbm.1, bf16[32,8192]{1,0:T(8,128)(2,1)} %do_hbm.1, bf16[32,1024]{1,0:T(8,128)(2,1)} %k_hbm.1, bf16[32,1024]{1,0:T(8,128)(2,1)} %v_hbm.1), custom_call_target="tpu_custom_call" | custom-call | tf_op jit(solution)/shard_map/gather/pallas_call | solution.py:422
  45.8 0.0 copy-start
  45.8 2.2 %copy-done = bf16[32,2,8,32,128]{4,3,2,1,0:T(8,128)(2,1)S(1)} copy-done((bf16[32,2,8,32,128]{4,3,2,1,0:T(8,128)(2,1)S(1)}, bf16[32,2,8,32,128]{4,3,2,1,0:T(8,128)(2,1)}, u32[]{:S(2)}) %copy-start) | copy-done | bytes 4194328
  48.0 0.0 copy-start.1
  48.0 1.0 copy-done.1
  49.0 0.0 copy-start.2
  49.0 1.0 copy-done.2
  50.1 0.0 copy-start.3
  50.1 0.7 copy-done.3
  50.7 0.0 copy-start.4
  50.7 0.7 copy-done.4
  51.4 11.9 %attention.1 = (bf16[2,256,512]{2,1,0:T(8,128)(2,1)S(1)}, bf16[2,256,512]{2,1,0:T(8,128)(2,1)S(1)}, bf16[32,2,128,256]{3,2,1,0:T(8,128)(2,1)S(1)}) custom-call(s32[32]{0:T(128)S(1)} %copy-done.3, s32[4]{0:T(128)S(1)} %copy-done.4, bf16[2,256,512]{2,1,0:T(8,128)(2,1)S(1)} %bitcast.10, bf16[2,256,512]{2,1,0:T(8,128)(2,1)S(1)} %bitcast.11, ...), custom_call_target="tpu_custom_call" | custom-call | tf_op jit(solution)/shard_map/attention/pallas_call | solution.py:232
  63.3 51.5 %scatter.1 = (bf16[32,8192]{1,0:T(8,128)(2,1)S(1)}, bf16[32,8192]{1,0:T(8,128)(2,1)S(1)}, bf16[32,1024]{1,0:T(8,128)(2,1)S(1)}, bf16[32,1024]{1,0:T(8,128)(2,1)S(1)}) custom-call(bf16[16,32,512]{2,1,0:T(8,128)(2,1)S(1)} %bitcast.8, bf16[16,32,512]{2,1,0:T(8,128)(2,1)S(1)} %bitcast.9, bf16[16,2,2,128,256]{4,3,2,1,0:T(8,128)(2,1)S(1)} %bitcast.6), custom_call_target="tpu_custom_call" | custom-call | tf_op jit(solution)/shard_map/scatter/pallas_call | solution.py:580
  114.8 1.0 settle.1
Async XLA Ops:
  45.8 2.2 %copy-start = (bf16[32,2,8,32,128]{4,3,2,1,0:T(8,128)(2,1)S(1)}, bf16[32,2,8,32,128]{4,3,2,1,0:T(8,128)(2,1)}, u32[]{:S(2)}) copy-start(bf16[32,2,8,32,128]{4,3,2,1,0:T(8,128)(2,1)} %get-tuple-element.16) | copy-start | bytes 12582916
  48.0 1.0 copy-start.1
  49.0 1.0 copy-start.2
  50.1 0.7 copy-start.3
  50.7 0.7 copy-start.4

commit v4 on v3

--- a/solution.py
+++ b/solution.py
@@ -25,25 +25,33 @@
 
 
 def attention_kernel(
-    span_ref, len_ref, q_v, do_v, kv_v,
+    span_hbm, len_hbm, q_v, do_v, kv_v,
     o_v, dq_v, dkv_v,
     holder, acc, probs, grads, wide_buf,
     q_t, do_t, q_s, do_s, o_acc, dq_acc, level_b, delta_b, starts,
+    span_ref, len_ref, table_sem,
 ):
+    load_span = pltpu.make_async_copy(span_hbm, span_ref, table_sem.at[0])
+    load_len = pltpu.make_async_copy(len_hbm, len_ref, table_sem.at[1])
+    load_span.start()
+    load_len.start()
     ctx = lax.axis_index("ctx")
     first_unit = ctx - ctx % UNITS
+
+    def clear(c, _):
+        acc[c] = jnp.zeros((2, WIDTH, SPAN), jnp.float32)
+        return 0
+
+    lax.fori_loop(0, N_CTX, clear, 0)
+
+    load_span.wait()
+    load_len.wait()
 
     def note(c, _):
         holder[span_ref[c]] = c
         return 0
 
     lax.fori_loop(0, N_CTX, note, 0)
-
-    def clear(c, _):
-        acc[c] = jnp.zeros((2, WIDTH, SPAN), jnp.float32)
-        return 0
-
-    lax.fori_loop(0, N_CTX, clear, 0)
 
     ends = []
     running = jnp.int32(0)
@@ -226,13 +234,13 @@
 def attention(q, do, kv, span_of, doc_lengths):
     rows = jax.ShapeDtypeStruct((UNITS, SPAN, UNIT_HEADS * WIDTH), jnp.bfloat16)
     blocks = jax.ShapeDtypeStruct((N_CTX, 2, WIDTH, SPAN), jnp.bfloat16)
-    smem = pl.BlockSpec(memory_space=pltpu.SMEM)
+    table = pl.BlockSpec(memory_space=pltpu.HBM)
     here = pl.BlockSpec(memory_space=pltpu.VMEM)
     vmem = pltpu.VMEM
     return pl.pallas_call(
         attention_kernel,
         out_shape=(rows, rows, blocks),
-        in_specs=[smem, smem, here, here, here],
+        in_specs=[table, table, here, here, here],
         out_specs=(here, here, here),
         scratch_shapes=[
             pltpu.SMEM((N_CTX,), jnp.int32),
@@ -249,6 +257,9 @@
             vmem((COLS, WIDTH), jnp.float32),
             vmem((COLS, WIDTH), jnp.float32),
             vmem((SPAN, WIDTH), jnp.int32),
+            pltpu.SMEM((N_CTX,), jnp.int32),
+            pltpu.SMEM((4,), jnp.int32),
+            pltpu.SemaphoreType.DMA((2,)),
         ],
         compiler_params=pltpu.CompilerParams(vmem_limit_bytes=40 * 1024 * 1024),
         name="attention",
@@ -340,7 +351,9 @@
         )
         own[-1].start()
 
-    def send_rows(src, dst, which):
+    rows_left = []
+
+    def start_rows(src, dst, which):
         def step_rows(step, _):
             peer = (mine + step) % group
             send(
@@ -349,13 +362,26 @@
             )
             return 0
 
-        lax.fori_loop(1, group, step_rows, 0)
+        rows_left.extend((step, step_rows) for step in range(1, group))
         copy = pltpu.make_async_copy(src.at[:, row_cols(mine)], dst.at[mine], local_sem.at[2 + which])
         copy.start()
         own.append(copy)
 
+    def send_some(count):
+        while rows_left and count > 0:
+            first, which = rows_left[0]
+            run = 0
+            while rows_left and run < count and rows_left[0][1] is which:
+                rows_left.pop(0)
+                run += 1
+            lax.fori_loop(first, first + run, which, 0)
+            count -= run
+
     loads[2].wait()
-    send_rows(q_in, q_out, 0)
+    start_rows(q_in, q_out, 0)
+    loads[3].wait()
+    start_rows(do_in, do_out, 1)
+    send_some(3)
     own[0].wait()
     own[1].wait()
     pieces = kv_out.at[ctx, :, pl.ds(0, heads - 1)]
@@ -377,8 +403,7 @@
     forward(ctx, right, right_recv.at[0, 0])
     forward(ctx, left, left_recv.at[0, 0])
     share(ctx)
-    loads[3].wait()
-    send_rows(do_in, do_out, 1)
+    send_some(4)
     arrived(kv_out.at[cross], cross_recv)
     forward(cross, right, right_recv.at[1, 0])
     forward(cross, left, left_recv.at[1, 0])
@@ -396,7 +421,9 @@
                 if d < reach[plane][way]:
                     forward(block, to, recv.at[plane, d])
                 share(block)
-
+                send_some(2)
+
+    send_some(len(rows_left))
     arrived(pieces, piece_send)
     for block, sem in sent:
         arrived(kv_out.at[block], sem)
@@ -416,7 +443,7 @@
     far = z_size // 2
     rows = jax.ShapeDtypeStruct((group, tokens, q.shape[1] // group), q.dtype)
     kv = jax.ShapeDtypeStruct((4 * z_size, 2, heads, tokens, WIDTH), q.dtype)
-    hbm = pl.BlockSpec(memory_space=pl.ANY)
+    hbm = pl.BlockSpec(memory_space=pltpu.HBM)
     here = pl.BlockSpec(memory_space=pltpu.VMEM)
     dma = pltpu.SemaphoreType.DMA
     return pl.pallas_call(
@@ -428,7 +455,7 @@
             dma((2,)), dma((2,)), dma, dma, dma((4 * far - 2 + 1,)), dma((2, far)), dma((2, far)),
             dma, dma, dma, dma((4,)), dma((4,)),
         ],
-        compiler_params=pltpu.CompilerParams(collective_id=0, has_side_effects=True, vmem_limit_bytes=58 * 1024 * 1024),
+        compiler_params=pltpu.CompilerParams(collective_id=0, has_side_effects=True, vmem_limit_bytes=32 * 1024 * 1024),
         name="gather",
     )(q, do, k, v)
 
@@ -480,20 +507,31 @@
 
     own = []
 
-    def send_rows(src, dst, which):
+    rows_left = []
+
+    def start_rows(src, dst, which):
         def step_rows(step, _):
             peer = (mine + step) % group
             send(
-                src.at[peer], dst.at[:, row_cols_mine],
+                src.at[peer], dst.at[:, row_cols(mine)],
                 row_send.at[which], row_recv.at[which], base + peer // heads, peer % heads,
             )
             return 0
 
-        row_cols_mine = row_cols(mine)
-        lax.fori_loop(1, group, step_rows, 0)
-        copy = pltpu.make_async_copy(src.at[mine], dst.at[:, row_cols_mine], local_sem.at[1 + which])
+        rows_left.extend((step, step_rows) for step in range(1, group))
+        copy = pltpu.make_async_copy(src.at[mine], dst.at[:, row_cols(mine)], local_sem.at[1 + which])
         copy.start()
         own.append(copy)
+
+    def send_some(count):
+        while rows_left and count > 0:
+            first, which = rows_left[0]
+            run = 0
+            while rows_left and run < count and rows_left[0][1] is which:
+                rows_left.pop(0)
+                run += 1
+            lax.fori_loop(first, first + run, which, 0)
+            count -= run
 
     def combine(block, extras, last=False):
         def add_half(side, _):
@@ -508,11 +546,11 @@
 
         lax.fori_loop(0, 2, add_half, 0)
 
+    start_rows(o_in, o_out, 0)
+    start_rows(dq_in, dq_out, 1)
     load.wait()
     sent = []
     for n, (plane, way, d, back) in enumerate(steps):
-        if n == min(4, len(steps) - 1):
-            send_rows(o_in, o_out, 0)
         block = order[n]
         recv, buf, to = ((right_recv, right_part, right), (left_recv, left_part, left))[way]
         arrived(twin_part.at[block], twin_recv.at[n])
@@ -523,8 +561,8 @@
         combine(block, extras)
         send(part.at[block], buf.at[plane, back], ring_send.at[n], recv.at[plane, back], to, head)
         sent.append((block, ring_send.at[n]))
-        if n == min(7, len(steps) - 1):
-            send_rows(dq_in, dq_out, 1)
+        send_some(3)
+    send_some(len(rows_left))
     for plane in (1, 0):
         n = len(steps) + 1 - plane
         block = order[n]
@@ -624,6 +662,10 @@
 
 
 def per_device(heads, z_size, queries, keys, values, output_gradient, doc_lengths, span_of):
+    queries, output_gradient, keys, values, doc_lengths, span_of = (
+        pltpu.with_memory_space_constraint(a, pltpu.HBM)
+        for a in (queries, output_gradient, keys, values, doc_lengths, span_of)
+    )
     q, do, kv = gather(queries, output_gradient, keys, values, z_size, heads)
     rows = (UNITS, SPAN, UNIT_HEADS * WIDTH)
     o, dq, dkv = attention(

time: 116 us -> 105 us (0.905)
  Pallas kernels: 110 us -> 104 us
  local copies, waits for them, and re-layouts: 5.57 us -> 0 us
    unnamed x10 -> x0, local copies, waits for them, and re-layouts: 5.57 us -> none
    pallas_call x1, Pallas kernels: 45.1 us -> 40.5 us  [gather(): pl.pallas_call(functools.partial(gather_kernel, z_size, heads), out_shape...]
where the time goes in v4:
time: 105 us; the launch traced here: 104 us
  Pallas kernels  104 us (99%)
    pallas_call x1, Pallas kernels, scatter(): pl.pallas_call(functools.partial(scatter_kernel, z_size, heads), out_shap...  50.5 us
    pallas_call x1, Pallas kernels, gather(): pl.pallas_call(functools.partial(gather_kernel, z_size, heads), out_shape...  40.5 us
    pallas_call x1, Pallas kernels, attention(): pl.pallas_call(attention_kernel, out_shape=(rows, rows, blocks), in_specs...  11.5 us

profile of v4, /device:TPU:2, one launch (start us, length us, event | category | flops | bytes accessed | tf_op | source)
XLA Modules:
  0.0 104.2 jit_solution(17040435874863950502)
XLA Ops:
  0.6 40.5 %gather.1 = (bf16[16,32,512]{2,1,0:T(8,128)(2,1)S(1)}, bf16[16,32,512]{2,1,0:T(8,128)(2,1)S(1)}, bf16[32,2,8,32,128]{4,3,2,1,0:T(8,128)(2,1)S(1)}) custom-call(bf16[32,8192]{1,0:T(8,128)(2,1)} %q_hbm.1, bf16[32,8192]{1,0:T(8,128)(2,1)} %do_hbm.1, bf16[32,1024]{1,0:T(8,128)(2,1)} %k_hbm.1, bf16[32,1024]{1,0:T(8,128)(2,1)} %v_hbm.1), custom_call_target="tpu_custom_call" | custom-call | tf_op jit(solution)/shard_map/gather/pallas_call | solution.py:449
  41.2 11.5 %attention.1 = (bf16[2,256,512]{2,1,0:T(8,128)(2,1)S(1)}, bf16[2,256,512]{2,1,0:T(8,128)(2,1)S(1)}, bf16[32,2,128,256]{3,2,1,0:T(8,128)(2,1)S(1)}) custom-call(s32[32]{0:T(128)} %span_hbm.1, s32[4]{0:T(128)} %len_hbm.1, bf16[2,256,512]{2,1,0:T(8,128)(2,1)S(1)} %bitcast.10, bf16[2,256,512]{2,1,0:T(8,128)(2,1)S(1)} %bitcast.11, ...), custom_call_target="tpu_custom_call" | custom-call | tf_op jit(solution)/shard_map/attention/pallas_call | solution.py:240
  52.7 50.5 %scatter.1 = (bf16[32,8192]{1,0:T(8,128)(2,1)S(1)}, bf16[32,8192]{1,0:T(8,128)(2,1)S(1)}, bf16[32,1024]{1,0:T(8,128)(2,1)S(1)}, bf16[32,1024]{1,0:T(8,128)(2,1)S(1)}) custom-call(bf16[16,32,512]{2,1,0:T(8,128)(2,1)S(1)} %bitcast.8, bf16[16,32,512]{2,1,0:T(8,128)(2,1)S(1)} %bitcast.9, bf16[16,2,2,128,256]{4,3,2,1,0:T(8,128)(2,1)S(1)} %bitcast.6), custom_call_target="tpu_custom_call" | custom-call | tf_op jit(solution)/shard_map/scatter/pallas_call | solution.py:618
  103.1 1.0 settle.1

commit v5 on v4

--- a/solution.py
+++ b/solution.py
@@ -27,7 +27,7 @@
 def attention_kernel(
     span_hbm, len_hbm, q_v, do_v, kv_v,
     o_v, dq_v, dkv_v,
-    holder, acc, probs, grads, wide_buf,
+    holder, slots, acc, probs, grads, wide_buf,
     q_t, do_t, q_s, do_s, o_acc, dq_acc, level_b, delta_b, starts,
     span_ref, len_ref, table_sem,
 ):
@@ -107,18 +107,17 @@
         def row_max(x):
             return jnp.broadcast_to(jnp.max(x, axis=1, keepdims=True), x.shape)
 
-        def forward(i, count, masked, take_top=False):
-            places = [holder[first_block + i + n] for n in range(count)]
-            for n, c in enumerate(places):
+        def score(slot, count):
+            for n in range(count):
                 wide_buf[n] = lax.dot_general(
-                    q_s[...], kv_v[c, 0], NT, preferred_element_type=jnp.float32
+                    q_s[...], kv_v[slots[slot + n], 0], NT, preferred_element_type=jnp.float32
                 )
-            if masked:
-                allowed = allowed_at(first_block + i)
+
+        def weigh(slot, count, allowed=None, take_top=False):
             for n in range(count):
                 for h in range(UNIT_HEADS):
                     s = wide_buf[n, rows_of(h)]
-                    if masked:
+                    if allowed is not None:
                         s = jnp.where(allowed, s, NEG)
                     if take_top:
                         level = row_max(halves_max(s))
@@ -126,30 +125,60 @@
                     else:
                         level = level_b[rows_of(h)]
                     p = jnp.exp2((s - both(level)) * LOG2_SCALE)
-                    probs[i + n, rows_of(h)] = p.astype(jnp.bfloat16)
-            values = below([beside([kv_v[c, 1], ones]) for c in places])
+                    probs[slot + n, rows_of(h)] = p.astype(jnp.bfloat16)
+
+        def attend(slot, count):
+            values = below([beside([kv_v[slots[slot + n], 1], ones]) for n in range(count)])
             o_acc[...] += jnp.dot(
-                beside([probs[i + n] for n in range(count)]), values, preferred_element_type=jnp.float32
+                beside([probs[slot + n] for n in range(count)]), values, preferred_element_type=jnp.float32
             )
 
         def masked_step(i, _):
-            forward(i, 1, True)
+            score(i, 1)
+            weigh(i, 1, allowed_at(first_block + i - 2))
             return 0
 
+        def attend_step(i, _):
+            attend(i, 1)
+            return 0
+
+        inner_from = edges + 2
+        inner = blocks - 1 - edges
+        slots[0] = first_unit
+        slots[1] = holder[span]
+
+        def place_slot(i, _):
+            slots[i + 2] = holder[first_block + i]
+            return 0
+
+        lax.fori_loop(0, blocks - 1, place_slot, 0)
+        probs[0] = jnp.zeros((COLS, SPAN), jnp.bfloat16)
         o_acc[...] = jnp.zeros_like(o_acc)
-        forward(blocks - 1, 1, True, take_top=True)
-        lax.fori_loop(0, edges, masked_step, 0)
-        inner = blocks - 1 - edges
+        score(1, 1)
+        weigh(1, 1, allowed_at(span), take_top=True)
+        lax.fori_loop(2, inner_from, masked_step, 0)
+        lax.fori_loop(1, edges, attend_step, 0)
 
         def pair_step(j, _):
-            forward(edges + 2 * j, 2, False)
+            slot = inner_from + 2 * j
+            score(slot, 2)
+            attend(slot - 2, 2)
+            weigh(slot, 2)
             return 0
 
         lax.fori_loop(0, inner // 2, pair_step, 0)
+        last = inner_from + inner - inner % 2
 
         @pl.when(inner % 2 == 1)
         def _():
-            forward(blocks - 2, 1, False)
+            score(last, 1)
+            attend(last - 2, 2)
+            weigh(last, 1)
+            attend(last, 1)
+
+        @pl.when(inner % 2 == 0)
+        def _():
+            attend(last - 2, 2)
 
         worst = jnp.max(jnp.where(o_acc[:, WIDTH:] < LIMIT, 0.0, 1.0))
 
@@ -159,18 +188,21 @@
             level_b[...] = jnp.full_like(level_b, NEG)
 
             def top_step(i, _):
-                k = kv_v[holder[first_block + i], 0]
-                allowed = allowed_at(first_block + i)
+                k = kv_v[slots[i], 0]
+                allowed = allowed_at(jnp.where(i == 1, span, first_block + i - 2))
                 for h in range(UNIT_HEADS):
                     s = lax.dot_general(q_s[rows_of(h)], k, NT, preferred_element_type=jnp.float32)
                     s = jnp.where(allowed, s, NEG)
                     level_b[rows_of(h)] = jnp.maximum(level_b[rows_of(h)], halves_max(s))
                 return 0
 
-            lax.fori_loop(0, blocks, top_step, 0)
+            lax.fori_loop(1, blocks + 1, top_step, 0)
             for h in range(UNIT_HEADS):
                 level_b[rows_of(h)] = row_max(level_b[rows_of(h)])
-            lax.fori_loop(0, blocks, masked_step, 0)
+            score(1, 1)
+            weigh(1, 1, allowed_at(span))
+            lax.fori_loop(2, blocks + 1, masked_step, 0)
+            lax.fori_loop(1, blocks + 1, attend_step, 0)
 
         for h in range(UNIT_HEADS):
             inverse = 1.0 / o_acc[rows_of(h), WIDTH:]
@@ -184,7 +216,7 @@
         dq_acc[...] = jnp.zeros_like(dq_acc)
 
         def backward(i, count):
-            places = [holder[first_block + i + n] for n in range(count)]
+            places = [slots[i + n] for n in range(count)]
             for n, c in enumerate(places):
                 wide_buf[n] = lax.dot_general(
                     do_s[...], kv_v[c, 1], NT, preferred_element_type=jnp.float32
@@ -208,14 +240,14 @@
                 acc[c, 1] += dv[:, part]
 
         def grad_step(j, _):
-            backward(2 * j, 2)
+            backward(2 * j + 1, 2)
             return 0
 
         lax.fori_loop(0, blocks // 2, grad_step, 0)
 
         @pl.when(blocks % 2 == 1)
         def _():
-            backward(blocks - 1, 1)
+            backward(blocks, 1)
 
         for h in range(UNIT_HEADS):
             dq_v[u, :, lanes_of(h)] = (dq_acc[rows_of(h)] * SCALE).astype(jnp.bfloat16)
@@ -244,6 +276,7 @@
         out_specs=(here, here, here),
         scratch_shapes=[
             pltpu.SMEM((N_CTX,), jnp.int32),
+            pltpu.SMEM((MAX_BLOCKS,), jnp.int32),
             vmem(blocks.shape, jnp.float32),
             vmem((MAX_BLOCKS, COLS, SPAN), jnp.bfloat16),
             vmem((2, COLS, SPAN), jnp.bfloat16),
@@ -480,9 +513,6 @@
     cross, twin = index(1 - x, z), base + 1 - core
     meet(group, ctx, head, core, heads, (right, left, cross))
 
-    load = pltpu.make_async_copy(dkv_in.at[:, core], part, local_sem.at[0])
-    load.start()
-
     far = z_size // 2
     reach = ((far, far - 1), (far - 1, far))
     steps = []
@@ -499,8 +529,14 @@
 
     order = [slot(plane, way, d) for plane, way, d, _ in steps]
     order += [slot(1, 0, 0), slot(0, 0, 0)]
-    for n, block in enumerate(order):
-        send(dkv_in.at[block, 1 - core], twin_part.at[block], twin_send, twin_recv.at[n], twin, head)
+    to_twin = list(enumerate(order))
+
+    def feed_twin(count):
+        for n, block in to_twin[:count]:
+            send(dkv_in.at[block, 1 - core], twin_part.at[block], twin_send, twin_recv.at[n], twin, head)
+        del to_twin[:count]
+
+    feed_twin(6)
 
     def row_cols(at):
         return pl.ds(pl.multiple_of(((at % heads) * 2 + at // heads) * wide, WIDTH), wide)
@@ -535,7 +571,7 @@
 
     def combine(block, extras, last=False):
         def add_half(side, _):
-            total = part[block, side].astype(jnp.float32) + twin_part[block, side].astype(jnp.float32)
+            total = dkv_in[block, core, side].astype(jnp.float32) + twin_part[block, side].astype(jnp.float32)
             for ref, at in extras:
                 total = total + ref[at + (side,)].astype(jnp.float32)
             if last:
@@ -548,7 +584,6 @@
 
     start_rows(o_in, o_out, 0)
     start_rows(dq_in, dq_out, 1)
-    load.wait()
     sent = []
     for n, (plane, way, d, back) in enumerate(steps):
         block = order[n]
@@ -561,7 +596,9 @@
         combine(block, extras)
         send(part.at[block], buf.at[plane, back], ring_send.at[n], recv.at[plane, back], to, head)
         sent.append((block, ring_send.at[n]))
+        feed_twin(1)
         send_some(3)
+    feed_twin(len(to_twin))
     send_some(len(rows_left))
     for plane in (1, 0):
         n = len(steps) + 1 - plane

time: 105 us -> 107 us (1.019)
  Pallas kernels: 104 us -> 106 us
    pallas_call x1, Pallas kernels: 11.5 us -> 12.7 us  [attention(): pl.pallas_call(attention_kernel, out_shape=(rows, rows, blocks), in_specs...]
    pallas_call x1, Pallas kernels: 50.5 us -> 51.7 us  [scatter(): pl.pallas_call(functools.partial(scatter_kernel, z_size, heads), out_shap...]
where the time goes in v5:
time: 107 us
  Pallas kernels  106 us (99%)
    pallas_call x1, Pallas kernels, scatter(): pl.pallas_call(functools.partial(scatter_kernel, z_size, heads), out_shap...  51.7 us
    pallas_call x1, Pallas kernels, gather(): pl.pallas_call(functools.partial(gather_kernel, z_size, heads), out_shape...  40.5 us
    pallas_call x1, Pallas kernels, attention(): pl.pallas_call(attention_kernel, out_shape=(rows, rows, blocks), in_specs...  12.7 us

profile of v5, /device:TPU:2, one launch (start us, length us, event | category | flops | bytes accessed | tf_op | source)
XLA Modules:
  0.0 106.6 jit_solution(7849171208039012506)
XLA Ops:
  0.6 40.5 %gather.1 = (bf16[16,32,512]{2,1,0:T(8,128)(2,1)S(1)}, bf16[16,32,512]{2,1,0:T(8,128)(2,1)S(1)}, bf16[32,2,8,32,128]{4,3,2,1,0:T(8,128)(2,1)S(1)}) custom-call(bf16[32,8192]{1,0:T(8,128)(2,1)} %q_hbm.1, bf16[32,8192]{1,0:T(8,128)(2,1)} %do_hbm.1, bf16[32,1024]{1,0:T(8,128)(2,1)} %k_hbm.1, bf16[32,1024]{1,0:T(8,128)(2,1)} %v_hbm.1), custom_call_target="tpu_custom_call" | custom-call | tf_op jit(solution)/shard_map/gather/pallas_call | solution.py:482
  41.2 12.7 %attention.1 = (bf16[2,256,512]{2,1,0:T(8,128)(2,1)S(1)}, bf16[2,256,512]{2,1,0:T(8,128)(2,1)S(1)}, bf16[32,2,128,256]{3,2,1,0:T(8,128)(2,1)S(1)}) custom-call(s32[32]{0:T(128)} %span_hbm.1, s32[4]{0:T(128)} %len_hbm.1, bf16[2,256,512]{2,1,0:T(8,128)(2,1)S(1)} %bitcast.10, bf16[2,256,512]{2,1,0:T(8,128)(2,1)S(1)} %bitcast.11, ...), custom_call_target="tpu_custom_call" | custom-call | tf_op jit(solution)/shard_map/attention/pallas_call | solution.py:272
  53.9 51.7 %scatter.1 = (bf16[32,8192]{1,0:T(8,128)(2,1)S(1)}, bf16[32,8192]{1,0:T(8,128)(2,1)S(1)}, bf16[32,1024]{1,0:T(8,128)(2,1)S(1)}, bf16[32,1024]{1,0:T(8,128)(2,1)S(1)}) custom-call(bf16[16,32,512]{2,1,0:T(8,128)(2,1)S(1)} %bitcast.8, bf16[16,32,512]{2,1,0:T(8,128)(2,1)S(1)} %bitcast.9, bf16[16,2,2,128,256]{4,3,2,1,0:T(8,128)(2,1)S(1)} %bitcast.6), custom_call_target="tpu_custom_call" | custom-call | tf_op jit(solution)/shard_map/scatter/pallas_call | solution.py:655
  105.5 1.0 settle.1

commit v6 on v5

--- a/solution.py
+++ b/solution.py
@@ -25,8 +25,8 @@
 
 
 def attention_kernel(
-    span_hbm, len_hbm, q_v, do_v, kv_v,
-    o_v, dq_v, dkv_v,
+    span_hbm, len_hbm, rows_v, kv_v,
+    out_v, dkv_v,
     holder, slots, acc, probs, grads, wide_buf,
     q_t, do_t, q_s, do_s, o_acc, dq_acc, level_b, delta_b, starts,
     span_ref, len_ref, table_sem,
@@ -83,6 +83,15 @@
     ones = jnp.ones((SPAN, WIDTH), jnp.bfloat16)
 
     def unit(u, _):
+        group = rows_v.shape[0] // UNITS
+        own = pl.ds(pl.multiple_of(u * group, group), group)
+
+        def head_rows(side, h):
+            return rows_v[own, side, :, lanes_of(h)].reshape(SPAN, WIDTH)
+
+        def put_rows(side, h, value):
+            out_v[own, side, :, lanes_of(h)] = value.astype(jnp.bfloat16).reshape(group, SPAN // group, WIDTH)
+
         span = span_ref[first_unit + u]
         first_pos = span * SPAN
         first_block = doc_start(first_pos) // SPAN
@@ -92,7 +101,7 @@
         starts[...] = doc_start(first_pos + lax.broadcasted_iota(jnp.int32, (SPAN, WIDTH), 0))
 
         for h in range(UNIT_HEADS):
-            q_h = q_v[u, :, lanes_of(h)]
+            q_h = head_rows(0, h)
             q_s[rows_of(h)] = q_h
             q_t[:, rows_of(h)] = q_h.T
 
@@ -207,8 +216,8 @@
         for h in range(UNIT_HEADS):
             inverse = 1.0 / o_acc[rows_of(h), WIDTH:]
             out = (o_acc[rows_of(h), :WIDTH] * inverse).astype(jnp.bfloat16)
-            o_v[u, :, lanes_of(h)] = out
-            scaled = (do_v[u, :, lanes_of(h)].astype(jnp.float32) * inverse).astype(jnp.bfloat16)
+            put_rows(0, h, out)
+            scaled = (head_rows(1, h).astype(jnp.float32) * inverse).astype(jnp.bfloat16)
             do_s[rows_of(h)] = scaled
             do_t[:, rows_of(h)] = scaled.T
             delta = jnp.sum(scaled.astype(jnp.float32) * out.astype(jnp.float32), axis=1, keepdims=True)
@@ -250,7 +259,7 @@
             backward(blocks, 1)
 
         for h in range(UNIT_HEADS):
-            dq_v[u, :, lanes_of(h)] = (dq_acc[rows_of(h)] * SCALE).astype(jnp.bfloat16)
+            put_rows(1, h, dq_acc[rows_of(h)] * SCALE)
         return 0
 
     lax.fori_loop(0, UNITS, unit, 0)
@@ -263,17 +272,16 @@
     lax.fori_loop(0, N_CTX, pack, 0)
 
 
-def attention(q, do, kv, span_of, doc_lengths):
-    rows = jax.ShapeDtypeStruct((UNITS, SPAN, UNIT_HEADS * WIDTH), jnp.bfloat16)
+def attention(rows, kv, span_of, doc_lengths):
     blocks = jax.ShapeDtypeStruct((N_CTX, 2, WIDTH, SPAN), jnp.bfloat16)
     table = pl.BlockSpec(memory_space=pltpu.HBM)
     here = pl.BlockSpec(memory_space=pltpu.VMEM)
     vmem = pltpu.VMEM
     return pl.pallas_call(
         attention_kernel,
-        out_shape=(rows, rows, blocks),
-        in_specs=[table, table, here, here, here],
-        out_specs=(here, here, here),
+        out_shape=(jax.ShapeDtypeStruct(rows.shape, rows.dtype), blocks),
+        in_specs=[table, table, here, here],
+        out_specs=(here, here),
         scratch_shapes=[
             pltpu.SMEM((N_CTX,), jnp.int32),
             pltpu.SMEM((MAX_BLOCKS,), jnp.int32),
@@ -296,7 +304,7 @@
         ],
         compiler_params=pltpu.CompilerParams(vmem_limit_bytes=40 * 1024 * 1024),
         name="attention",
-    )(span_of, doc_lengths, q, do, kv)
+    )(span_of, doc_lengths, rows, kv)
 
 
 MESH_IDS = pl.DeviceIdType.MESH
@@ -337,24 +345,30 @@
 
 def gather_kernel(
     z_size, heads,
-    q_hbm, do_hbm, k_hbm, v_hbm, q_out, do_out, kv_out, q_in, do_in, k_in, v_in,
+    q_hbm, do_hbm, k_hbm, v_hbm, rows_out, kv_out, rows_in, pieces_in,
     row_send, row_recv, piece_send, piece_recv, ring_send, right_recv, left_recv,
     cross_recv, twin_send, twin_recv, local_sem, load_sem,
 ):
     loads = []
-    for n, (src, dst) in enumerate(((k_hbm, k_in), (v_hbm, v_in), (q_hbm, q_in), (do_hbm, do_in))):
+    for n, (src, dst) in enumerate((
+        (k_hbm, pieces_in.at[0]), (v_hbm, pieces_in.at[1]), (q_hbm, rows_in.at[0]), (do_hbm, rows_in.at[1])
+    )):
         loads.append(pltpu.make_async_copy(src, dst, load_sem.at[n]))
         loads[-1].start()
     ctx, head, x, z, core = place(z_size)
     group = 2 * heads
     base = ctx - core
     mine = core * heads + head
-    wide = q_in.shape[1] // group
+    wide = rows_in.shape[2] // group
 
     def index(x_at, z_at):
         return (x_at * z_size + z_at) * 2 + core
 
-    right, left = index(x, (z + 1) % z_size), index(x, (z + z_size - 1) % z_size)
+    def block(x_at, z_at):
+        return kv_out.at[x_at, z_at * 2 + core]
+
+    right_z, left_z = (z + 1) % z_size, (z + z_size - 1) % z_size
+    right, left = index(x, right_z), index(x, left_z)
     cross, twin = index(1 - x, z), base + 1 - core
     meet(group, ctx, head, core, heads, (right, left, cross))
 
@@ -365,82 +379,67 @@
         peer_core, peer_head = at // heads, at % heads
         return pl.ds(pl.multiple_of((peer_head * 2 + peer_core) * wide, WIDTH), wide)
 
+    mine_block = block(x, z)
+
     def send_pieces(step, _):
         peer = (head + step) % heads
-        for side, ref in enumerate((k_in, v_in)):
-            send(
-                ref.at[:, piece_cols(peer)], kv_out.at[ctx, side, head],
-                piece_send, piece_recv, ctx, peer,
-            )
+        send(pieces_in.at[:, :, piece_cols(peer)], mine_block.at[:, head], piece_send, piece_recv, ctx, peer)
         return 0
 
     loads[0].wait()
     loads[1].wait()
     lax.fori_loop(1, heads, send_pieces, 0)
-    own = []
-    for side, ref in enumerate((k_in, v_in)):
-        own.append(
-            pltpu.make_async_copy(ref.at[:, piece_cols(head)], kv_out.at[ctx, side, head], local_sem.at[side])
+    own_piece = pltpu.make_async_copy(
+        pieces_in.at[:, :, piece_cols(head)], mine_block.at[:, head], local_sem.at[0]
+    )
+    own_piece.start()
+    loads[2].wait()
+    loads[3].wait()
+    own_rows = pltpu.make_async_copy(rows_in.at[:, :, row_cols(mine)], rows_out.at[mine], local_sem.at[1])
+    own_rows.start()
+
+    def send_row(step, _):
+        peer = (mine + step) % group
+        send(
+            rows_in.at[:, :, row_cols(peer)], rows_out.at[mine], row_send, row_recv,
+            base + peer // heads, peer % heads,
         )
-        own[-1].start()
-
-    rows_left = []
-
-    def start_rows(src, dst, which):
-        def step_rows(step, _):
-            peer = (mine + step) % group
-            send(
-                src.at[:, row_cols(peer)], dst.at[mine],
-                row_send.at[which], row_recv.at[which], base + peer // heads, peer % heads,
-            )
-            return 0
-
-        rows_left.extend((step, step_rows) for step in range(1, group))
-        copy = pltpu.make_async_copy(src.at[:, row_cols(mine)], dst.at[mine], local_sem.at[2 + which])
-        copy.start()
-        own.append(copy)
-
-    def send_some(count):
-        while rows_left and count > 0:
-            first, which = rows_left[0]
-            run = 0
-            while rows_left and run < count and rows_left[0][1] is which:
-                rows_left.pop(0)
-                run += 1
-            lax.fori_loop(first, first + run, which, 0)
-            count -= run
-
-    loads[2].wait()
-    start_rows(q_in, q_out, 0)
-    loads[3].wait()
-    start_rows(do_in, do_out, 1)
-    send_some(3)
-    own[0].wait()
-    own[1].wait()
-    pieces = kv_out.at[ctx, :, pl.ds(0, heads - 1)]
+        return 0
+
+    rows_sent = [1]
+
+    def send_rows(count):
+        stop = min(rows_sent[0] + count, group)
+        lax.fori_loop(rows_sent[0], stop, send_row, 0)
+        rows_sent[0] = stop
+
+    send_rows(2)
+    own_piece.wait()
+    pieces = mine_block.at[:, pl.ds(0, heads - 1)]
     arrived(pieces, piece_recv)
 
     sent = []
 
-    def forward(block, to, recv):
+    def forward(what, to, recv):
         sem = ring_send.at[len(sent)]
-        send(kv_out.at[block], kv_out.at[block], sem, recv, to, head)
-        sent.append((block, sem))
-
-    def share(block):
-        send(kv_out.at[block], kv_out.at[block], twin_send, twin_recv, twin, head)
+        send(what, what, sem, recv, to, head)
+        sent.append((what, sem))
+
+    def share(z_at):
+        both_x = kv_out.at[:, z_at * 2 + core]
+        send(both_x, both_x, twin_send, twin_recv, twin, head)
 
     far = z_size // 2
     reach = ((far, far - 1), (far - 1, far))
-    forward(ctx, cross, cross_recv)
-    forward(ctx, right, right_recv.at[0, 0])
-    forward(ctx, left, left_recv.at[0, 0])
-    share(ctx)
-    send_some(4)
-    arrived(kv_out.at[cross], cross_recv)
-    forward(cross, right, right_recv.at[1, 0])
-    forward(cross, left, left_recv.at[1, 0])
-    share(cross)
+    forward(mine_block, cross, cross_recv)
+    forward(mine_block, right, right_recv.at[0, 0])
+    forward(mine_block, left, left_recv.at[0, 0])
+    send_rows(2)
+    cross_block = block(1 - x, z)
+    arrived(cross_block, cross_recv)
+    forward(cross_block, right, right_recv.at[1, 0])
+    forward(cross_block, left, left_recv.at[1, 0])
+    share(z)
     for d in range(1, far + 1):
         for plane in range(2):
             at_x = x if plane == 0 else 1 - x
@@ -449,53 +448,55 @@
                     continue
                 recv, to = ((right_recv, right), (left_recv, left))[way]
                 origin = (z + z_size - d) % z_size if way == 0 else (z + d) % z_size
-                block = index(at_x, origin)
-                arrived(kv_out.at[block], recv.at[plane, d - 1])
+                what = block(at_x, origin)
+                arrived(what, recv.at[plane, d - 1])
                 if d < reach[plane][way]:
-                    forward(block, to, recv.at[plane, d])
-                share(block)
-                send_some(2)
-
-    send_some(len(rows_left))
+                    forward(what, to, recv.at[plane, d])
+                if plane == 1:
+                    share(origin)
+                send_rows(1)
+
+    send_rows(group)
     arrived(pieces, piece_send)
-    for block, sem in sent:
-        arrived(kv_out.at[block], sem)
-    half = kv_out.at[pl.ds(0, 2 * z_size)]
-    arrived(half, twin_send)
-    arrived(half, twin_recv)
-    for which, dst in enumerate((q_out, do_out)):
-        own[2 + which].wait()
-        rows = dst.at[pl.ds(0, group - 1)]
-        arrived(rows, row_send.at[which])
-        arrived(rows, row_recv.at[which])
+    for what, sem in sent:
+        arrived(what, sem)
+    arrived(kv_out.at[0], twin_send)
+    arrived(kv_out.at[0], twin_recv)
+    own_rows.wait()
+    rows = rows_out.at[pl.ds(0, group - 1)]
+    arrived(rows, row_send)
+    arrived(rows, row_recv)
 
 
 def gather(q, do, k, v, z_size, heads):
     tokens = q.shape[0]
     group = 2 * heads
     far = z_size // 2
-    rows = jax.ShapeDtypeStruct((group, tokens, q.shape[1] // group), q.dtype)
-    kv = jax.ShapeDtypeStruct((4 * z_size, 2, heads, tokens, WIDTH), q.dtype)
+    rows = jax.ShapeDtypeStruct((group, 2, tokens, q.shape[1] // group), q.dtype)
+    kv = jax.ShapeDtypeStruct((2, 2 * z_size, 2, heads, tokens, WIDTH), q.dtype)
     hbm = pl.BlockSpec(memory_space=pltpu.HBM)
     here = pl.BlockSpec(memory_space=pltpu.VMEM)
     dma = pltpu.SemaphoreType.DMA
     return pl.pallas_call(
         functools.partial(gather_kernel, z_size, heads),
-        out_shape=(rows, rows, kv),
+        out_shape=(rows, kv),
         in_specs=[hbm] * 4,
-        out_specs=(here, here, here),
-        scratch_shapes=[pltpu.VMEM(a.shape, a.dtype) for a in (q, do, k, v)] + [
-            dma((2,)), dma((2,)), dma, dma, dma((4 * far - 2 + 1,)), dma((2, far)), dma((2, far)),
-            dma, dma, dma, dma((4,)), dma((4,)),
+        out_specs=(here, here),
+        scratch_shapes=[
+            pltpu.VMEM((2,) + q.shape, q.dtype), pltpu.VMEM((2,) + k.shape, k.dtype),
+            dma, dma, dma, dma, dma((4 * far - 2 + 1,)), dma((2, far)), dma((2, far)),
+            dma, dma, dma, dma((2,)), dma((4,)),
         ],
-        compiler_params=pltpu.CompilerParams(collective_id=0, has_side_effects=True, vmem_limit_bytes=32 * 1024 * 1024),
+        compiler_params=pltpu.CompilerParams(
+            collective_id=0, has_side_effects=True, vmem_limit_bytes=32 * 1024 * 1024
+        ),
         name="gather",
     )(q, do, k, v)
 
 
 def scatter_kernel(
     z_size, heads,
-    o_in, dq_in, dkv_in, o_out, dq_out, dk_out, dv_out,
+    rows_in, dkv_in, rows_out, pieces_out,
     part, twin_part, right_part, left_part, cross_part, final,
     row_send, row_recv, piece_send, piece_recv, ring_send, right_recv, left_recv,
     cross_recv, twin_send, twin_recv, local_sem,
@@ -504,7 +505,7 @@
     group = 2 * heads
     base = ctx - core
     mine = core * heads + head
-    wide = o_in.shape[2]
+    wide = rows_in.shape[3]
 
     def index(x_at, z_at):
         return (x_at * z_size + z_at) * 2 + core
@@ -522,88 +523,81 @@
             if d > 0:
                 steps.append((plane, way, d, back))
 
-    def slot(plane, way, d):
-        at_x = x if plane == 0 else 1 - x
-        at_z = (z + d) % z_size if way == 0 else (z + z_size - d) % z_size
-        return at_x * z_size + at_z
-
-    order = [slot(plane, way, d) for plane, way, d, _ in steps]
-    order += [slot(1, 0, 0), slot(0, 0, 0)]
-    to_twin = list(enumerate(order))
+    to_twin = [far] + [s * d for d in range(far - 1, 0, -1) for s in (1, -1)] + [0]
+    place_of = {offset: n for n, offset in enumerate(to_twin)}
+    fed, had = [0], [0]
+
+    def z_of(offset):
+        return (z + z_size + offset) % z_size
 
     def feed_twin(count):
-        for n, block in to_twin[:count]:
-            send(dkv_in.at[block, 1 - core], twin_part.at[block], twin_send, twin_recv.at[n], twin, head)
-        del to_twin[:count]
-
-    feed_twin(6)
-
-    def row_cols(at):
-        return pl.ds(pl.multiple_of(((at % heads) * 2 + at // heads) * wide, WIDTH), wide)
-
-    own = []
-
-    rows_left = []
-
-    def start_rows(src, dst, which):
-        def step_rows(step, _):
-            peer = (mine + step) % group
-            send(
-                src.at[peer], dst.at[:, row_cols(mine)],
-                row_send.at[which], row_recv.at[which], base + peer // heads, peer % heads,
-            )
-            return 0
-
-        rows_left.extend((step, step_rows) for step in range(1, group))
-        copy = pltpu.make_async_copy(src.at[mine], dst.at[:, row_cols(mine)], local_sem.at[1 + which])
-        copy.start()
-        own.append(copy)
-
-    def send_some(count):
-        while rows_left and count > 0:
-            first, which = rows_left[0]
-            run = 0
-            while rows_left and run < count and rows_left[0][1] is which:
-                rows_left.pop(0)
-                run += 1
-            lax.fori_loop(first, first + run, which, 0)
-            count -= run
-
-    def combine(block, extras, last=False):
+        for n in range(fed[0], min(fed[0] + count, len(to_twin))):
+            at = z_of(to_twin[n])
+            send(dkv_in.at[:, at, 1 - core], twin_part.at[:, at], twin_send, twin_recv.at[n], twin, head)
+        fed[0] = min(fed[0] + count, len(to_twin))
+
+    def need_twin(offset):
+        n = place_of[far if abs(offset) == far else offset]
+        while had[0] <= n:
+            arrived(twin_part.at[:, z_of(to_twin[had[0]])], twin_recv.at[had[0]])
+            had[0] += 1
+
+    feed_twin(3)
+    my_rows = pl.ds(pl.multiple_of((head * 2 + core) * wide, WIDTH), wide)
+
+    def send_row(step, _):
+        peer = (mine + step) % group
+        send(
+            rows_in.at[peer], rows_out.at[:, :, my_rows], row_send, row_recv,
+            base + peer // heads, peer % heads,
+        )
+        return 0
+
+    rows_sent = [1]
+
+    def send_rows(count):
+        stop = min(rows_sent[0] + count, group)
+        lax.fori_loop(rows_sent[0], stop, send_row, 0)
+        rows_sent[0] = stop
+
+    own_rows = pltpu.make_async_copy(rows_in.at[mine], rows_out.at[:, :, my_rows], local_sem.at[0])
+    own_rows.start()
+
+    def combine(at_x, at_z, extras, last=False):
         def add_half(side, _):
-            total = dkv_in[block, core, side].astype(jnp.float32) + twin_part[block, side].astype(jnp.float32)
+            total = dkv_in[at_x, at_z, core, side].astype(jnp.float32)
+            total = total + twin_part[at_x, at_z, side].astype(jnp.float32)
             for ref, at in extras:
                 total = total + ref[at + (side,)].astype(jnp.float32)
             if last:
                 final[side] = total.T.astype(final.dtype).reshape(final.shape[1:])
             else:
-                part[block, side] = total.astype(part.dtype)
+                part[at_x, at_z, side] = total.astype(part.dtype)
             return 0
 
         lax.fori_loop(0, 2, add_half, 0)
 
-    start_rows(o_in, o_out, 0)
-    start_rows(dq_in, dq_out, 1)
     sent = []
     for n, (plane, way, d, back) in enumerate(steps):
-        block = order[n]
+        offset = d if way == 0 else -d
+        at_x, at_z = (x if plane == 0 else 1 - x), z_of(offset)
         recv, buf, to = ((right_recv, right_part, right), (left_recv, left_part, left))[way]
-        arrived(twin_part.at[block], twin_recv.at[n])
+        need_twin(offset)
         extras = []
         if back > 0:
             arrived(buf.at[plane, back - 1], recv.at[plane, back - 1])
             extras = [(buf, (plane, back - 1))]
-        combine(block, extras)
-        send(part.at[block], buf.at[plane, back], ring_send.at[n], recv.at[plane, back], to, head)
-        sent.append((block, ring_send.at[n]))
-        feed_twin(1)
-        send_some(3)
+        combine(at_x, at_z, extras)
+        send(part.at[at_x, at_z], buf.at[plane, back], ring_send.at[n], recv.at[plane, back], to, head)
+        sent.append((part.at[at_x, at_z], ring_send.at[n]))
+        if n % 2 == 0:
+            feed_twin(1)
+        send_rows(1)
     feed_twin(len(to_twin))
-    send_some(len(rows_left))
+    send_rows(group)
+    need_twin(0)
     for plane in (1, 0):
-        n = len(steps) + 1 - plane
-        block = order[n]
-        arrived(twin_part.at[block], twin_recv.at[n])
+        at_x = x if plane == 0 else 1 - x
         last_right, last_left = reach[plane][0] - 1, reach[plane][1] - 1
         arrived(right_part.at[plane, last_right], right_recv.at[plane, last_right])
         arrived(left_part.at[plane, last_left], left_recv.at[plane, last_left])
@@ -611,75 +605,71 @@
         if plane == 0:
             arrived(cross_part.at[0], cross_recv)
             extras.append((cross_part, (0,)))
-        combine(block, extras, last=plane == 0)
+        combine(at_x, z, extras, last=plane == 0)
         if plane == 1:
-            send(part.at[block], cross_part.at[0], ring_send.at[n], cross_recv, cross, head)
-            sent.append((block, ring_send.at[n]))
+            sem = ring_send.at[len(steps)]
+            send(part.at[at_x, z], cross_part.at[0], sem, cross_recv, cross, head)
+            sent.append((part.at[at_x, z], sem))
 
     my_cols = pl.ds(pl.multiple_of(head * WIDTH, WIDTH), WIDTH)
 
     def send_pieces(step, _):
         peer = (head + step) % heads
-        for side, dst in enumerate((dk_out, dv_out)):
-            send(final.at[side, peer], dst.at[:, my_cols], piece_send, piece_recv.at[side], ctx, peer)
+        send(final.at[:, peer], pieces_out.at[:, :, my_cols], piece_send, piece_recv, ctx, peer)
         return 0
 
     lax.fori_loop(1, heads, send_pieces, 0)
-    for side, dst in enumerate((dk_out, dv_out)):
-        copy = pltpu.make_async_copy(final.at[side, head], dst.at[:, my_cols], local_sem.at[3 + side])
-        copy.start()
-        own.append(copy)
-
-    for copy in own:
-        copy.wait()
-    for block, sem in sent:
-        arrived(part.at[block], sem)
-    arrived(part.at[pl.ds(0, 2 * z_size)], twin_send)
-    for which, dst in enumerate((o_out, dq_out)):
-        rows = dst.at[:, pl.ds(0, (group - 1) * wide)]
-        arrived(rows, row_send.at[which])
-        arrived(rows, row_recv.at[which])
+    own_piece = pltpu.make_async_copy(final.at[:, head], pieces_out.at[:, :, my_cols], local_sem.at[1])
+    own_piece.start()
+    own_piece.wait()
+    own_rows.wait()
+    for what, sem in sent:
+        arrived(what, sem)
+    arrived(part, twin_send)
+    rows = rows_out.at[:, :, pl.ds(0, (group - 1) * wide)]
+    arrived(rows, row_send)
+    arrived(rows, row_recv)
     arrived(final.at[:, pl.ds(0, heads - 1)], piece_send)
-    for side, dst in enumerate((dk_out, dv_out)):
-        arrived(dst.at[:, pl.ds(0, (heads - 1) * WIDTH)], piece_recv.at[side])
-
-
-def scatter(o, dq, dkv, z_size, heads):
-    group, tokens, wide = o.shape
+    arrived(pieces_out.at[:, :, pl.ds(0, (heads - 1) * WIDTH)], piece_recv)
+
+
+def scatter(rows, dkv, z_size, heads):
+    group, _, tokens, wide = rows.shape
     far = z_size // 2
-    rows = jax.ShapeDtypeStruct((tokens, group * wide), o.dtype)
-    pieces = jax.ShapeDtypeStruct((tokens, heads * WIDTH), o.dtype)
-    block = dkv.shape[2:]
+    block = dkv.shape[3:]
     here = pl.BlockSpec(memory_space=pltpu.VMEM)
     dma = pltpu.SemaphoreType.DMA
     return pl.pallas_call(
         functools.partial(scatter_kernel, z_size, heads),
-        out_shape=(rows, rows, pieces, pieces),
-        in_specs=[here] * 3,
-        out_specs=(here,) * 4,
+        out_shape=(
+            jax.ShapeDtypeStruct((2, tokens, group * wide), rows.dtype),
+            jax.ShapeDtypeStruct((2, tokens, heads * WIDTH), rows.dtype),
+        ),
+        in_specs=[here] * 2,
+        out_specs=(here, here),
         scratch_shapes=[
-            pltpu.VMEM((2 * z_size,) + block, dkv.dtype),
-            pltpu.VMEM((2 * z_size,) + block, dkv.dtype),
+            pltpu.VMEM((2, z_size) + block, dkv.dtype),
+            pltpu.VMEM((2, z_size) + block, dkv.dtype),
             pltpu.VMEM((2, far) + block, dkv.dtype),
             pltpu.VMEM((2, far) + block, dkv.dtype),
             pltpu.VMEM((1,) + block, dkv.dtype),
             pltpu.VMEM((2, heads, tokens, WIDTH), dkv.dtype),
-            dma((2,)), dma((2,)), dma, dma((2,)), dma((4 * far - 2 + 1,)), dma((2, far)), dma((2, far)),
-            dma, dma, dma((2 * z_size,)), dma((5,)),
+            dma, dma, dma, dma, dma((4 * far - 2 + 1,)), dma((2, far)), dma((2, far)),
+            dma, dma, dma((z_size,)), dma((2,)),
         ],
         compiler_params=pltpu.CompilerParams(
             collective_id=1, has_side_effects=True, vmem_limit_bytes=24 * 1024 * 1024
         ),
         name="scatter",
-    )(o, dq, dkv)
-
-
-def settle_kernel(*refs):
-    count = len(refs) // 2
-    sem = refs[-1]
-    copies = [pltpu.make_async_copy(refs[i], refs[count + i], sem.at[i]) for i in range(count)]
-    for copy in copies:
-        copy.start()
+    )(rows, dkv)
+
+
+def settle_kernel(rows, pieces, o, dq, dk, dv, sem):
+    copies = []
+    for src, outs in ((rows, (o, dq)), (pieces, (dk, dv))):
+        for n, out in enumerate(outs):
+            copies.append(pltpu.make_async_copy(src.at[n], out, sem.at[len(copies)]))
+            copies[-1].start()
     for copy in copies:
         copy.wait()
 
@@ -689,10 +679,10 @@
     here = pl.BlockSpec(memory_space=pltpu.VMEM)
     return pl.pallas_call(
         settle_kernel,
-        out_shape=tuple(jax.ShapeDtypeStruct(a.shape, a.dtype) for a in arrays),
+        out_shape=tuple(jax.ShapeDtypeStruct(a.shape[1:], a.dtype) for a in arrays for _ in range(2)),
         in_specs=[here] * len(arrays),
-        out_specs=(hbm,) * len(arrays),
-        scratch_shapes=[pltpu.SemaphoreType.DMA((len(arrays),))],
+        out_specs=(hbm,) * 4,
+        scratch_shapes=[pltpu.SemaphoreType.DMA((4,))],
         compiler_params=pltpu.CompilerParams(vmem_limit_bytes=32 * 1024 * 1024),
         name="settle",
     )(*arrays)
@@ -703,13 +693,9 @@
         pltpu.with_memory_space_constraint(a, pltpu.HBM)
         for a in (queries, output_gradient, keys, values, doc_lengths, span_of)
     )
-    q, do, kv = gather(queries, output_gradient, keys, values, z_size, heads)
-    rows = (UNITS, SPAN, UNIT_HEADS * WIDTH)
-    o, dq, dkv = attention(
-        q.reshape(rows), do.reshape(rows), kv.reshape(N_CTX, 2, SPAN, WIDTH), span_of, doc_lengths
-    )
-    dkv = dkv.reshape((N_CTX // 2, 2) + dkv.shape[1:])
-    return settle(scatter(o.reshape(q.shape), dq.reshape(q.shape), dkv, z_size, heads))
+    rows, kv = gather(queries, output_gradient, keys, values, z_size, heads)
+    outs, dkv = attention(rows, kv.reshape(N_CTX, 2, SPAN, WIDTH), span_of, doc_lengths)
+    return settle(scatter(outs, dkv.reshape((2, z_size, 2) + dkv.shape[1:]), z_size, heads))
 
 
 def solution(mesh):

time: 107 us -> 110 us (1.028)
  Pallas kernels: 106 us -> 108 us
    pallas_call x1, Pallas kernels: 51.7 us -> 56.9 us  [scatter(): pl.pallas_call(functools.partial(scatter_kernel, z_size, heads), out_shap...]
    pallas_call x1, Pallas kernels: 12.7 us -> 10.9 us  [attention(): pl.pallas_call(attention_kernel, out_shape=(jax.ShapeDtypeStruct(rows.sha...]
    pallas_call x1, Pallas kernels: 40.5 us -> 39 us  [gather(): pl.pallas_call(functools.partial(gather_kernel, z_size, heads), out_shape...]
where the time goes in v6:
time: 110 us; the launch traced here: 108 us
  Pallas kernels  108 us (98%)
    pallas_call x1, Pallas kernels, scatter(): pl.pallas_call(functools.partial(scatter_kernel, z_size, heads), out_shap...  56.9 us
    pallas_call x1, Pallas kernels, gather(): pl.pallas_call(functools.partial(gather_kernel, z_size, heads), out_shape...  39 us
    pallas_call x1, Pallas kernels, attention(): pl.pallas_call(attention_kernel, out_shape=(jax.ShapeDtypeStruct(rows.sha...  10.9 us

profile of v6, /device:TPU:2, one launch (start us, length us, event | category | flops | bytes accessed | tf_op | source)
XLA Modules:
  0.0 108.5 jit_solution(7634908810708306067)
XLA Ops:
  0.6 39.0 %gather.1 = (bf16[16,2,32,512]{3,2,1,0:T(8,128)(2,1)S(1)}, bf16[2,16,2,8,32,128]{5,4,3,2,1,0:T(8,128)(2,1)S(1)}) custom-call(bf16[32,8192]{1,0:T(8,128)(2,1)} %q_hbm.1, bf16[32,8192]{1,0:T(8,128)(2,1)} %do_hbm.1, bf16[32,1024]{1,0:T(8,128)(2,1)} %k_hbm.1, bf16[32,1024]{1,0:T(8,128)(2,1)} %v_hbm.1), custom_call_target="tpu_custom_call" | custom-call | tf_op jit(solution)/shard_map/gather/pallas_call | solution.py:480
  39.7 10.9 %attention.1 = (bf16[16,2,32,512]{3,2,1,0:T(8,128)(2,1)S(1)}, bf16[32,2,128,256]{3,2,1,0:T(8,128)(2,1)S(1)}) custom-call(s32[32]{0:T(128)} %span_hbm.1, s32[4]{0:T(128)} %len_hbm.1, bf16[16,2,32,512]{3,2,1,0:T(8,128)(2,1)S(1)} %get-tuple-element.10.rows_v, bf16[32,2,256,128]{3,2,1,0:T(8,128)(2,1)S(1)} %bitcast.3), custom_call_target="tpu_custom_call" | custom-call | tf_op jit(solution)/shard_map/attention/pallas_call | solution.py:280
  50.5 56.9 %scatter.1 = (bf16[2,32,8192]{2,1,0:T(8,128)(2,1)S(1)}, bf16[2,32,1024]{2,1,0:T(8,128)(2,1)S(1)}) custom-call(bf16[16,2,32,512]{3,2,1,0:T(8,128)(2,1)S(1)} %get-tuple-element.12.rows_in, bf16[2,8,2,2,128,256]{5,4,3,2,1,0:T(8,128)(2,1)S(1)} %bitcast.2), custom_call_target="tpu_custom_call" | custom-call | tf_op jit(solution)/shard_map/scatter/pallas_call | solution.py:642
  107.5 1.0 settle.1
